TPU v7x, 256 devices: a whole 4x4x8 slice. The times are simulated.
256 devices in a mesh: group: 8 (over z_hi, core), gx: 4 (over x), gy: 8 (over y, z_lo).
Axes of the slice: x: 4, y: 4, z: 8 (z_hi: 4, z_lo: 2; z = z_hi * 2 + z_lo), core: 2. Of those that a mesh axis runs over, the one named last changes fastest.
Arguments:
- start_vectors: float32 [8, 4, 8, 8, 384, 128], P('group', 'gx', 'gy')
- tile_blocks: bfloat16 [8, 4, 8, 8, 4, 384, 384], P('group', 'gx', 'gy')
- block_columns: int32 [8, 4, 8, 8, 4], P('group', 'gx', 'gy'), may hold values from 0 to 11, as said below
- sleeve_rod: int32 [4, 8, 7, 8, 8], P('gx', 'gy'), may hold values from -1 to 511, as said below
- sleeve_membrane: int32 [4, 8, 7, 8, 8], P('gx', None, None, 'gy'), may hold values from -1 to 511, as said below
- sleeve_stiffness: float32 [4, 8, 7, 8, 8], P('gx', None, None, 'gy'), may hold values from 0.25 to 4
Outputs:
- final_vectors: float32 [8, 4, 8, 8, 384, 128], P('group', 'gx', 'gy')
- norms: float32 [3, 128], replicated
Inputs may be any that keep to these rules, and one draw needn't show every extreme that they name: `block_columns`: entry 0 of block row r is r itself; every other entry names one of the device's 8 blocks, or 8 to 11 for the west, east, south and north ghost blocks. sleeve_rod[x, y, m, y2, :] lists the nodes of rod device (0, x, y) tied to membrane tile (m + 1, x, y2); -1 marks an empty slot and live slots come first. In every draw one membrane tile receives 8 live slots from each of the 8 rod devices of its column. `sleeve_membrane`: -1 at exactly the slots where sleeve_rod is -1; elsewhere a node of membrane tile (m + 1, x, y2).
All inputs are finite; a program needn't handle non-finite values.
Results may differ from a plain program's by a relative error of at most 0.005.
Values may be sent and summed in bfloat16 or wider, within the bound.
No kernel may reach another device: no remote copies, remote signals or barrier semaphores. Data moves between devices by JAX's collectives and lax.ppermute only.
A program may use at most 64 MiB of HBM per device.

v0:
```python
import jax
import jax.numpy as jnp
from jax import lax
from jax.sharding import PartitionSpec as P

MATVECS = 3


epsilon = 1e-06


def extended_2(shard, sides, width):
    for axis, dim in sides:
        count, length = (lax.axis_size(axis), shard.shape[dim])
        up = [(i, (i + 1) % count) for i in range(count - 1)]
        down = [(j, i) for i, j in up]
        last = lax.slice_in_dim(shard, length - width, length, axis=dim)
        initial = lax.slice_in_dim(shard, 0, width, axis=dim)
        before = lax.ppermute(last, axis, up)
        after = lax.ppermute(initial, axis, down)
        shard = jnp.concatenate([before, shard, after], axis=dim)
    return shard


def local(start_vectors, tile_blocks, block_columns, sleeve_rod, sleeve_membrane, sleeve_stiffness):
    n_blocks = tile_blocks.shape[3]
    width = tile_blocks.shape[5]
    vectors = start_vectors.shape[5]
    capacity = sleeve_rod.shape[4]
    groups = lax.axis_size("group")
    rows_y = lax.axis_size("gy")
    nodes = n_blocks * width // 6
    payload = 6 * vectors
    all_dofs = float(groups * lax.axis_size("gx") * rows_y * n_blocks * width)
    group_index = lax.axis_index("group")
    rod_flag = group_index == 0
    membrane_flag = (group_index > 0).astype(jnp.float32)
    blocks = tile_blocks[0, 0, 0]
    columns = block_columns[0, 0, 0].reshape(-1)
    send_nodes = sleeve_rod[0, 0].reshape(-1)
    send_live = (send_nodes >= 0) & rod_flag
    send_safe = jnp.maximum(send_nodes, 0)
    node_ids = jnp.arange(nodes, dtype=jnp.int32)
    rod_gather = jnp.where(
        (node_ids[:, None] == send_nodes[None, :]) & rod_flag, jnp.float32(1.0), jnp.float32(0.0)
    )
    memb_slot = jnp.maximum(group_index - 1, 0)
    recv_nodes = lax.dynamic_index_in_dim(
        sleeve_membrane[0, :, :, 0, :], memb_slot, axis=1, keepdims=False
    ).reshape(-1)
    recv_stiff = lax.dynamic_index_in_dim(
        sleeve_stiffness[0, :, :, 0, :], memb_slot, axis=1, keepdims=False
    ).reshape(-1)
    recv_live = (recv_nodes >= 0).astype(jnp.float32) * membrane_flag
    recv_safe = jnp.maximum(recv_nodes, 0)
    weighted = (
        jnp.where(node_ids[:, None] == recv_nodes[None, :], recv_stiff[None, :], jnp.float32(0.0))
        * membrane_flag
    )
    node_weight = jnp.sum(weighted, axis=1)
    slot_stiff = recv_stiff * recv_live
    current = start_vectors[0, 0, 0]
    norms = []
    for matvec in range(MATVECS):
        rounded = current.astype(jnp.bfloat16)
        edges_x = jnp.stack([rounded[0], rounded[n_blocks - 1]])
        padded_x = extended_2(edges_x, (("gx", 0),), 1)
        edges_y = jnp.stack([rounded[n_blocks - 2], rounded[1]])
        padded_y = extended_2(edges_y, (("gy", 0),), 1)
        extended = jnp.concatenate(
            [rounded, padded_x[0:1], padded_x[3:4], padded_y[0:1], padded_y[3:4]], axis=0
        )
        picked = jnp.take(extended, columns, axis=0).reshape(n_blocks, -1, width, vectors)
        product = jnp.einsum("rkij,rkjs->ris", blocks, picked, preferred_element_type=jnp.float32)
        node_rows = rounded.reshape(nodes, payload)
        outgoing = jnp.where(
            send_live[:, None], jnp.take(node_rows, send_safe, axis=0), jnp.zeros((), jnp.bfloat16)
        )
        outgoing = outgoing.reshape(groups - 1, rows_y, capacity, payload)
        outgoing = jnp.concatenate(
            [jnp.zeros((1, rows_y, capacity, payload), jnp.bfloat16), outgoing], axis=0
        )
        arrived = lax.all_to_all(
            outgoing.reshape(groups * rows_y, capacity, payload),
            ("group", "gy"),
            split_axis=0,
            concat_axis=0,
            tiled=True,
        )[:rows_y]
        arrived = arrived.reshape(rows_y * capacity, payload).astype(jnp.float32)
        pulled = jnp.dot(weighted, arrived, precision=lax.Precision.HIGHEST)
        coupling = node_weight[:, None] * node_rows.astype(jnp.float32) - pulled
        memb_at_slot = jnp.take(node_rows, recv_safe, axis=0).astype(jnp.float32)
        delta = (slot_stiff[:, None] * (memb_at_slot - arrived)).astype(jnp.bfloat16)
        back = delta.reshape(1, rows_y, capacity, payload)
        back = jnp.concatenate(
            [back, jnp.zeros((groups - 1, rows_y, capacity, payload), jnp.bfloat16)], axis=0
        )
        returned = lax.all_to_all(
            back.reshape(groups * rows_y, capacity, payload),
            ("group", "gy"),
            split_axis=0,
            concat_axis=0,
            tiled=True,
        )
        returned = (
            returned.reshape(groups, rows_y * capacity, payload)[1:]
            .reshape(-1, payload)
            .astype(jnp.float32)
        )
        pushed = jnp.dot(rod_gather, returned, precision=lax.Precision.HIGHEST)
        coupling = coupling - pushed
        coupled = product + coupling.reshape(n_blocks, width, vectors)
        squares = lax.psum(jnp.sum(coupled * coupled, axis=(0, 1)), ("group", "gx", "gy"))
        scale = jnp.sqrt(squares / all_dofs + epsilon)
        current = coupled / scale
        norms.append(scale)
    return (current[None, None, None], jnp.stack(norms))


def solution(mesh):
    return jax.shard_map(
        local,
        mesh=mesh,
        in_specs=(
            P("group", "gx", "gy", None, None, None),
            P("group", "gx", "gy", None, None, None, None),
            P("group", "gx", "gy", None, None),
            P("gx", "gy", None, None, None),
            P("gx", None, None, "gy", None),
            P("gx", None, None, "gy", None),
        ),
        out_specs=(P("group", "gx", "gy", None, None, None), P()),
        check_vma=False,
    )
```

profile of v0, /device:TPU:1, one launch (start us, length us, event | category | flops | bytes accessed | tf_op | source)
XLA Modules:
  0.0 512.0 jit_solution(3302803746197962856)
XLA Ops:
  7.2 13.3 %all-to-all-start = ((bf16[64,8,768]{2,1,0:T(8,128)(2,1)}), bf16[64,8,768]{2,1,0:T(8,128)(2,1)}, u32[]{:S(2)}, u32[]{:S(2)}) async-start(bf16[64,8,768]{2,1,0:T(8,128)(2,1)} %bitcast.108), calls=%async_computation | async-start | bytes 1572864 | tf_op jit(solution)/shard_map/all_to_all | solution.py:83
  22.5 4.0 collective-permute-start.2
  27.8 4.6 collective-permute-start
  34.3 9.4 %all-to-all-done = bf16[64,8,768]{2,1,0:T(8,128)(2,1)} async-done(((bf16[64,8,768]{2,1,0:T(8,128)(2,1)}), bf16[64,8,768]{2,1,0:T(8,128)(2,1)}, u32[]{:S(2)}, u32[]{:S(2)}) %all-to-all-start) | async-done | bytes 786464 | tf_op jit(solution)/shard_map/all_to_all | solution.py:83
  45.6 5.7 %all-to-all-start.1 = ((bf16[64,8,768]{2,1,0:T(8,128)(2,1)}), bf16[64,8,768]{2,1,0:T(8,128)(2,1)S(1)}, u32[]{:S(2)}, u32[]{:S(2)}) async-start(bf16[64,8,768]{2,1,0:T(8,128)(2,1)} %bitcast.14), calls=%async_computation.1 | async-start | bytes 1572864 | tf_op jit(solution)/shard_map/all_to_all | solution.py:99
  55.1 3.9 broadcast_select_fusion.2
  61.9 12.4 %all-to-all-done.1 = bf16[64,8,768]{2,1,0:T(8,128)(2,1)S(1)} async-done(((bf16[64,8,768]{2,1,0:T(8,128)(2,1)}), bf16[64,8,768]{2,1,0:T(8,128)(2,1)S(1)}, u32[]{:S(2)}, u32[]{:S(2)}) %all-to-all-start.1) | async-done | bytes 786464 | tf_op jit(solution)/shard_map/all_to_all | solution.py:99
  74.4 3.2 subtract_subtract_fusion.2
  82.0 8.3 %multiply_reduce_fusion.2 = (f32[128]{0:T(128)S(1)}, f32[8,384,128]{1,2,0:T(8,128)}) fusion(f32[8,384,128]{1,2,0:T(8,128)} %copy.24, bf16[8,4,384,128]{3,2,1,0:T(8,128)(2,1)S(1)} %bitcast.103, bf16[1,1,1,8,4,384,384]{6,5,4,3,2,1,0:T(8,128)(2,1)} %param.13), kind=kOutput, calls=%fused_computation.34 | convolution fusion | flops 1209139072 | bytes 15729152 | tf_op jit(solution)/shard_map/rkij,rkjs->ris/dot_general | solution.py:74
  90.3 75.8 %psum.21 = f32[128]{0:T(128)S(1)} all-reduce(f32[128]{0:T(128)S(1)} %get-tuple-element.37), channel_id=1, replica_groups=mesh['group'=8,'gx'=4,'gy'=8] {'group','gx','gy'}, use_global_device_ids=true, to_apply=%region_2.6 | all-reduce | flops 128 | bytes 1024 | tf_op jit(solution)/shard_map/psum | solution.py:114
  174.1 6.7 %all-to-all-start.2 = ((bf16[64,8,768]{2,1,0:T(8,128)(2,1)}), bf16[64,8,768]{2,1,0:T(8,128)(2,1)}, u32[]{:S(2)}, u32[]{:S(2)}) async-start(bf16[64,8,768]{2,1,0:T(8,128)(2,1)} %bitcast.110), calls=%async_computation.2 | async-start | bytes 1572864 | tf_op jit(solution)/shard_map/all_to_all | solution.py:83
  181.5 22.2 %all-to-all-done.2 = bf16[64,8,768]{2,1,0:T(8,128)(2,1)} async-done(((bf16[64,8,768]{2,1,0:T(8,128)(2,1)}), bf16[64,8,768]{2,1,0:T(8,128)(2,1)}, u32[]{:S(2)}, u32[]{:S(2)}) %all-to-all-start.2) | async-done | bytes 786464 | tf_op jit(solution)/shard_map/all_to_all | solution.py:83
  205.7 6.2 %all-to-all-start.3 = ((bf16[64,8,768]{2,1,0:T(8,128)(2,1)}), bf16[64,8,768]{2,1,0:T(8,128)(2,1)}, u32[]{:S(2)}, u32[]{:S(2)}) async-start(bf16[64,8,768]{2,1,0:T(8,128)(2,1)} %bitcast.107), calls=%async_computation.3 | async-start | bytes 1572864 | tf_op jit(solution)/shard_map/all_to_all | solution.py:99
  215.4 4.0 collective-permute-start.6
  220.7 4.4 collective-permute-done.5
  225.2 4.3 collective-permute-done.6
  229.5 3.3 collective-permute-done.7
  235.5 4.0 broadcast_select_fusion
  242.4 3.4 subtract_subtract_fusion.1
  250.2 8.2 %multiply_reduce_fusion.1 = (f32[128]{0:T(128)S(1)}, f32[8,384,128]{1,2,0:T(8,128)}) fusion(f32[8,384,128]{1,2,0:T(8,128)} %copy.26, bf16[8,4,384,128]{2,3,1,0:T(8,128)(2,1)S(1)} %bitcast.105, bf16[1,1,1,8,4,384,384]{6,5,4,3,2,1,0:T(8,128)(2,1)} %param.13), kind=kOutput, calls=%fused_computation.31 | convolution fusion | flops 1209139072 | bytes 15729152 | tf_op jit(solution)/shard_map/rkij,rkjs->ris/dot_general | solution.py:74
  258.4 77.9 %psum.22 = f32[128]{0:T(128)S(1)} all-reduce(f32[128]{0:T(128)S(1)} %get-tuple-element.39), channel_id=1, replica_groups=mesh['group'=8,'gx'=4,'gy'=8] {'group','gx','gy'}, use_global_device_ids=true, to_apply=%region_4.8 | all-reduce | flops 128 | bytes 1024 | tf_op jit(solution)/shard_map/psum | solution.py:114
  344.3 8.2 %all-to-all-start.4 = ((bf16[64,8,768]{2,1,0:T(8,128)(2,1)}), bf16[64,8,768]{2,1,0:T(8,128)(2,1)}, u32[]{:S(2)}, u32[]{:S(2)}) async-start(bf16[64,8,768]{2,1,0:T(8,128)(2,1)} %bitcast.109), calls=%async_computation.4 | async-start | bytes 1572864 | tf_op jit(solution)/shard_map/all_to_all | solution.py:83
  353.2 22.2 %all-to-all-done.4 = bf16[64,8,768]{2,1,0:T(8,128)(2,1)} async-done(((bf16[64,8,768]{2,1,0:T(8,128)(2,1)}), bf16[64,8,768]{2,1,0:T(8,128)(2,1)}, u32[]{:S(2)}, u32[]{:S(2)}) %all-to-all-start.4) | async-done | bytes 786464 | tf_op jit(solution)/shard_map/all_to_all | solution.py:83
  377.4 6.2 %all-to-all-start.5 = ((bf16[64,8,768]{2,1,0:T(8,128)(2,1)}), bf16[64,8,768]{2,1,0:T(8,128)(2,1)}, u32[]{:S(2)}, u32[]{:S(2)}) async-start(bf16[64,8,768]{2,1,0:T(8,128)(2,1)} %bitcast.106), calls=%async_computation.5 | async-start | bytes 1572864 | tf_op jit(solution)/shard_map/all_to_all | solution.py:99
  387.1 4.0 collective-permute-start.10
  392.4 4.4 collective-permute-done.9
  396.9 4.3 collective-permute-done.10
  401.2 3.3 collective-permute-done.11
  407.2 4.0 broadcast_select_fusion.1
  414.1 3.4 subtract_subtract_fusion
  421.9 8.2 %multiply_reduce_fusion = (f32[128]{0:T(128)S(1)}, f32[8,384,128]{1,2,0:T(8,128)}) fusion(f32[8,384,128]{1,2,0:T(8,128)} %copy.28, bf16[8,4,384,128]{2,3,1,0:T(8,128)(2,1)S(1)} %bitcast.104, bf16[1,1,1,8,4,384,384]{6,5,4,3,2,1,0:T(8,128)(2,1)} %param.13), kind=kOutput, calls=%fused_computation.28 | convolution fusion | flops 1209139072 | bytes 15729152 | tf_op jit(solution)/shard_map/rkij,rkjs->ris/dot_general | solution.py:74
  430.1 77.6 %psum.23 = f32[128]{0:T(128)S(1)} all-reduce(f32[128]{0:T(128)S(1)} %get-tuple-element.41), channel_id=1, replica_groups=mesh['group'=8,'gx'=4,'gy'=8] {'group','gx','gy'}, use_global_device_ids=true, to_apply=%region_6.10 | all-reduce | flops 128 | bytes 1024 | tf_op jit(solution)/shard_map/psum | solution.py:114
  (105 shorter events, 79.2 us)
Async XLA Ops:
  0.6 32.0 %copy-start = (s32[1,8,7,1,8]{4,3,2,1,0:T(1,128)S(1)}, s32[1,8,7,1,8]{4,3,2,1,0:T(1,128)}, u32[]{:S(2)}) copy-start(s32[1,8,7,1,8]{4,3,2,1,0:T(1,128)} %param.16) | copy-start | bytes 5380
  6.3 26.2 %copy-start.5 = (s32[1,1,1,8,4]{3,4,2,1,0:T(4,128)S(1)}, s32[1,1,1,8,4]{3,4,2,1,0:T(4,128)}, u32[]{:S(2)}) copy-start(s32[1,1,1,8,4]{3,4,2,1,0:T(4,128)} %param.14) | copy-start | bytes 388
  7.2 36.4 %all-to-all-start = ((bf16[64,8,768]{2,1,0:T(8,128)(2,1)}), bf16[64,8,768]{2,1,0:T(8,128)(2,1)}, u32[]{:S(2)}, u32[]{:S(2)}) async-start(bf16[64,8,768]{2,1,0:T(8,128)(2,1)} %bitcast.108), calls=%async_computation | async-start | bytes 1572864 | tf_op jit(solution)/shard_map/all_to_all | solution.py:83
  21.2 31.2 %collective-permute-start.3 = (bf16[1,384,128]{2,1,0:T(8,128)(2,1)S(1)}, bf16[1,384,128]{2,1,0:T(8,128)(2,1)S(1)}, u32[]{:S(2)}, u32[]{:S(2)}) collective-permute-start(bf16[1,384,128]{2,1,0:T(8,128)(2,1)S(1)} %get-tuple-element.25), channel_id=1, source_target_pairs={{1,0},{2,1},{3,2},{4,3},{5,4},{6,5},{7,6},{9,8},{10,9},{11,10},{12... | collective-permute-start | bytes 294920 | tf_op jit(solution)/shard_map/ppermute | solution.py:20
  22.5 29.9 %collective-permute-start.2 = (bf16[1,384,128]{2,1,0:T(8,128)(2,1)S(1)}, bf16[1,384,128]{2,1,0:T(8,128)(2,1)S(1)}, u32[]{:S(2)}, u32[]{:S(2)}) collective-permute-start(bf16[1,384,128]{2,1,0:T(8,128)(2,1)S(1)} %get-tuple-element.26), channel_id=1, source_target_pairs={{0,1},{1,2},{2,3},{3,4},{4,5},{5,6},{6,7},{8,9},{9,10},{10,11},{11... | collective-permute-start | bytes 294920 | tf_op jit(solution)/shard_map/ppermute | solution.py:19
  26.5 25.9 %collective-permute-start.1 = (bf16[1,384,128]{2,1,0:T(8,128)(2,1)S(1)}, bf16[1,384,128]{2,1,0:T(8,128)(2,1)S(1)}, u32[]{:S(2)}, u32[]{:S(2)}) collective-permute-start(bf16[1,384,128]{2,1,0:T(8,128)(2,1)S(1)} %get-tuple-element.27), channel_id=1, source_target_pairs={{8,0},{16,8},{24,16},{9,1},{17,9},{25,17},{10,2},{18,10},{26,18},{... | collective-permute-start | bytes 294920 | tf_op jit(solution)/shard_map/ppermute | solution.py:20
  27.8 23.7 %collective-permute-start = (bf16[1,384,128]{2,1,0:T(8,128)(2,1)}, bf16[1,384,128]{2,1,0:T(8,128)(2,1)}, u32[]{:S(2)}, u32[]{:S(2)}) collective-permute-start(bf16[1,384,128]{2,1,0:T(8,128)(2,1)} %get-tuple-element.28), channel_id=1, source_target_pairs={{0,8},{8,16},{16,24},{1,9},{9,17},{17,25},{2,10},{10,18},{18,26},{... | collective-permute-start | bytes 294920 | tf_op jit(solution)/shard_map/ppermute | solution.py:19
  45.6 28.8 %all-to-all-start.1 = ((bf16[64,8,768]{2,1,0:T(8,128)(2,1)}), bf16[64,8,768]{2,1,0:T(8,128)(2,1)S(1)}, u32[]{:S(2)}, u32[]{:S(2)}) async-start(bf16[64,8,768]{2,1,0:T(8,128)(2,1)} %bitcast.14), calls=%async_computation.1 | async-start | bytes 1572864 | tf_op jit(solution)/shard_map/all_to_all | solution.py:99
  78.8 3.2 copy-start.2
  174.1 29.6 %all-to-all-start.2 = ((bf16[64,8,768]{2,1,0:T(8,128)(2,1)}), bf16[64,8,768]{2,1,0:T(8,128)(2,1)}, u32[]{:S(2)}, u32[]{:S(2)}) async-start(bf16[64,8,768]{2,1,0:T(8,128)(2,1)} %bitcast.110), calls=%async_computation.2 | async-start | bytes 1572864 | tf_op jit(solution)/shard_map/all_to_all | solution.py:83
  205.7 36.7 %all-to-all-start.3 = ((bf16[64,8,768]{2,1,0:T(8,128)(2,1)}), bf16[64,8,768]{2,1,0:T(8,128)(2,1)}, u32[]{:S(2)}, u32[]{:S(2)}) async-start(bf16[64,8,768]{2,1,0:T(8,128)(2,1)} %bitcast.107), calls=%async_computation.3 | async-start | bytes 1572864 | tf_op jit(solution)/shard_map/all_to_all | solution.py:99
  212.0 8.7 %collective-permute-start.4 = (bf16[1,384,128]{1,2,0:T(8,128)(2,1)S(1)}, bf16[1,384,128]{1,2,0:T(8,128)(2,1)S(1)}, u32[]{:S(2)}, u32[]{:S(2)}) collective-permute-start(bf16[1,384,128]{1,2,0:T(8,128)(2,1)S(1)} %get-tuple-element.24), channel_id=1, source_target_pairs={{0,8},{8,16},{16,24},{1,9},{9,17},{17,25},{2,10},{10,18},{18,26},{... | collective-permute-start | bytes 294920 | tf_op jit(solution)/shard_map/ppermute | solution.py:19
  214.1 18.7 %collective-permute-start.7 = (bf16[1,384,128]{1,2,0:T(8,128)(2,1)S(1)}, bf16[1,384,128]{1,2,0:T(8,128)(2,1)S(1)}, u32[]{:S(2)}, u32[]{:S(2)}) collective-permute-start(bf16[1,384,128]{1,2,0:T(8,128)(2,1)S(1)} %get-tuple-element.21), channel_id=1, source_target_pairs={{1,0},{2,1},{3,2},{4,3},{5,4},{6,5},{7,6},{9,8},{10,9},{11,10},{12... | collective-permute-start | bytes 294920 | tf_op jit(solution)/shard_map/ppermute | solution.py:20
  215.4 14.1 %collective-permute-start.6 = (bf16[1,384,128]{1,2,0:T(8,128)(2,1)S(1)}, bf16[1,384,128]{1,2,0:T(8,128)(2,1)S(1)}, u32[]{:S(2)}, u32[]{:S(2)}) collective-permute-start(bf16[1,384,128]{1,2,0:T(8,128)(2,1)S(1)} %get-tuple-element.22), channel_id=1, source_target_pairs={{0,1},{1,2},{2,3},{3,4},{4,5},{5,6},{6,7},{8,9},{9,10},{10,11},{11... | collective-permute-start | bytes 294920 | tf_op jit(solution)/shard_map/ppermute | solution.py:19
  219.4 5.8 %collective-permute-start.5 = (bf16[1,384,128]{1,2,0:T(8,128)(2,1)S(1)}, bf16[1,384,128]{1,2,0:T(8,128)(2,1)S(1)}, u32[]{:S(2)}, u32[]{:S(2)}) collective-permute-start(bf16[1,384,128]{1,2,0:T(8,128)(2,1)S(1)} %get-tuple-element.23), channel_id=1, source_target_pairs={{8,0},{16,8},{24,16},{9,1},{17,9},{25,17},{10,2},{18,10},{26,18},{... | collective-permute-start | bytes 294920 | tf_op jit(solution)/shard_map/ppermute | solution.py:20
  247.0 3.2 copy-start.4
  344.3 31.2 %all-to-all-start.4 = ((bf16[64,8,768]{2,1,0:T(8,128)(2,1)}), bf16[64,8,768]{2,1,0:T(8,128)(2,1)}, u32[]{:S(2)}, u32[]{:S(2)}) async-start(bf16[64,8,768]{2,1,0:T(8,128)(2,1)} %bitcast.109), calls=%async_computation.4 | async-start | bytes 1572864 | tf_op jit(solution)/shard_map/all_to_all | solution.py:83
  377.4 36.7 %all-to-all-start.5 = ((bf16[64,8,768]{2,1,0:T(8,128)(2,1)}), bf16[64,8,768]{2,1,0:T(8,128)(2,1)}, u32[]{:S(2)}, u32[]{:S(2)}) async-start(bf16[64,8,768]{2,1,0:T(8,128)(2,1)} %bitcast.106), calls=%async_computation.5 | async-start | bytes 1572864 | tf_op jit(solution)/shard_map/all_to_all | solution.py:99
  383.7 8.7 %collective-permute-start.8 = (bf16[1,384,128]{1,2,0:T(8,128)(2,1)S(1)}, bf16[1,384,128]{1,2,0:T(8,128)(2,1)S(1)}, u32[]{:S(2)}, u32[]{:S(2)}) collective-permute-start(bf16[1,384,128]{1,2,0:T(8,128)(2,1)S(1)} %get-tuple-element.20), channel_id=1, source_target_pairs={{0,8},{8,16},{16,24},{1,9},{9,17},{17,25},{2,10},{10,18},{18,26},{... | collective-permute-start | bytes 294920 | tf_op jit(solution)/shard_map/ppermute | solution.py:19
  385.8 18.7 %collective-permute-start.11 = (bf16[1,384,128]{1,2,0:T(8,128)(2,1)S(1)}, bf16[1,384,128]{1,2,0:T(8,128)(2,1)S(1)}, u32[]{:S(2)}, u32[]{:S(2)}) collective-permute-start(bf16[1,384,128]{1,2,0:T(8,128)(2,1)S(1)} %get-tuple-element.17), channel_id=1, source_target_pairs={{1,0},{2,1},{3,2},{4,3},{5,4},{6,5},{7,6},{9,8},{10,9},{11,10},{12... | collective-permute-start | bytes 294920 | tf_op jit(solution)/shard_map/ppermute | solution.py:20
  387.1 14.1 %collective-permute-start.10 = (bf16[1,384,128]{1,2,0:T(8,128)(2,1)S(1)}, bf16[1,384,128]{1,2,0:T(8,128)(2,1)S(1)}, u32[]{:S(2)}, u32[]{:S(2)}) collective-permute-start(bf16[1,384,128]{1,2,0:T(8,128)(2,1)S(1)} %get-tuple-element.18), channel_id=1, source_target_pairs={{0,1},{1,2},{2,3},{3,4},{4,5},{5,6},{6,7},{8,9},{9,10},{10,11},{11... | collective-permute-start | bytes 294920 | tf_op jit(solution)/shard_map/ppermute | solution.py:19
  391.1 5.8 %collective-permute-start.9 = (bf16[1,384,128]{1,2,0:T(8,128)(2,1)S(1)}, bf16[1,384,128]{1,2,0:T(8,128)(2,1)S(1)}, u32[]{:S(2)}, u32[]{:S(2)}) collective-permute-start(bf16[1,384,128]{1,2,0:T(8,128)(2,1)S(1)} %get-tuple-element.19), channel_id=1, source_target_pairs={{8,0},{16,8},{24,16},{9,1},{17,9},{25,17},{10,2},{18,10},{26,18},{... | collective-permute-start | bytes 294920 | tf_op jit(solution)/shard_map/ppermute | solution.py:20
  418.7 3.2 copy-start.3
  507.8 3.8 copy-start.1
where the time goes:
time: 522 us; the launch traced here: 512 us
  blocking collectives  231 us (44%)
  waiting for transfers between devices  90.3 us (17%)
  starting transfers between devices  75 us (14%)
  local copies, waits for them, and re-layouts  47.3 us (9%)
  matrix products  43.6 us (8%)
  other arithmetic  22.9 us (4%)
    psum x3, blocking collectives, local(): lax.psum(jnp.sum(coupled * coupled, axis=(0, 1)), ('group', 'gx', 'gy'))  231 us
    all_to_all x3, waiting for transfers between devices, local(): lax.all_to_all(outgoing.reshape(groups * rows_y, capacity, payload), ('gr...  53.8 us
    all_to_all x3, starting transfers between devices, local(): lax.all_to_all(outgoing.reshape(groups * rows_y, capacity, payload), ('gr...  28.2 us
    dot_general x3, matrix products, local(): jnp.einsum('rkij,rkjs->ris', blocks, picked, preferred_element_type=jnp.f...  24.7 us
    ppermute x6, starting transfers between devices, extended_2(): before = lax.ppermute(last, axis, up)  20.9 us
    all_to_all x3, starting transfers between devices, local(): lax.all_to_all(back.reshape(groups * rows_y, capacity, payload), ('group'...  18.2 us
    ppermute x6, waiting for transfers between devices, extended_2(): after = lax.ppermute(initial, axis, down)  15.4 us
    reshape x6, local copies, waits for them, and re-layouts, local(): coupled = product + coupling.reshape(n_blocks, width, vectors)  13.3 us
  transfers between devices with their start and end apart: 18, of which 10 were waited for; matrix products, arithmetic and copies ran while one was open for 7% of the time, Pallas kernels for 0%

commit v1 on v0

v1 whole, which is shorter than its diff:
```python
import functools

import jax
import jax.numpy as jnp
from jax import lax
from jax.experimental import pallas as pl
from jax.experimental.pallas import tpu as pltpu
from jax.sharding import Mesh, PartitionSpec as P

MATVECS = 3
TILE = 384
NB = 8
KB = 4
S = 128
CAP = 8
DOFS = 6
NODES = NB * TILE // DOFS
ROWS = NB * TILE
GY_N = 8
PAIRS = 4
SLOTS = 7 * GY_N * CAP
MSLOTS = GY_N * CAP
ROWS_MSG = DOFS * CAP
EPS = 1e-06
ALL_DOFS = 8 * 4 * 8 * ROWS

GROUP = ("zh", "core")
GY = ("y", "zl")
EVERY = ("zh", "core", "gx", "y", "zl")
ORDER = (0, 1, 3, 5, 2, 4, 6)

VMEM = pl.BlockSpec(memory_space=pltpu.VMEM)
SMEM = pl.BlockSpec(memory_space=pltpu.SMEM)
BF16 = jnp.bfloat16
F32 = jnp.float32


def dot(a, b):
    return jnp.dot(a, b, preferred_element_type=F32)


def update_kernel(first, last, *refs):
    refs = list(refs)
    take = lambda n: [refs.pop(0) for _ in range(n)]
    (rod, base) = take(2)
    if not first:
        (inv, recv_a, recv_b, own_a, own_b, kappa, scatter) = take(7)
    if not last:
        (gather,) = take(1)
        (rounded, east, west, north, south, send_a, send_b) = take(7)
    else:
        (y,) = take(1)
    if not first:
        (squares,) = take(1)
    (slots,) = take(1)
    if not last:
        (y,) = take(1)
    is_rod = rod[0] == 1

    if not first:
        own = [own_b.at[0], own_a.at[1], own_a.at[2], own_a.at[3], own_b.at[1], own_b.at[2], own_b.at[3]]
        other = [recv_a.at[0], recv_a.at[1], recv_a.at[2], recv_a.at[3], recv_b.at[0], recv_b.at[1], recv_b.at[2]]

        def difference(q, mine, theirs):
            gap = mine[...].astype(F32) - theirs[...].astype(F32)
            stiff = kappa[q * MSLOTS : (q + 1) * MSLOTS].reshape(GY_N, 1, CAP, S)
            slots[q * GY_N : (q + 1) * GY_N] = gap.reshape(GY_N, DOFS, CAP, S) * stiff

        @pl.when(is_rod)
        def _():
            for q in range(7):
                difference(q, own[q], other[q])

        @pl.when(jnp.logical_not(is_rod))
        def _():
            difference(0, own_a.at[0], recv_a.at[0])
            slots[GY_N : 2 * GY_N] = jnp.zeros((GY_N, DOFS, CAP, S), F32)

        scale = inv[...]

        def finish(d, coupling):
            value = (base[pl.ds(d, NODES, stride=DOFS), :] + coupling) * scale
            y[pl.ds(d, NODES, stride=DOFS), :] = value
            part = jnp.sum(jnp.square(value).reshape(NODES // 8, 8, S), axis=0)
            return jnp.sum(part, axis=0, keepdims=True)

        @pl.when(is_rod)
        def _():
            total = jnp.zeros((1, S), F32)
            for d in range(DOFS):
                delta = slots[:, d].reshape(SLOTS, S)
                total += finish(d, dot(scatter[...], delta.astype(BF16)))
            squares[...] = total

        @pl.when(jnp.logical_not(is_rod))
        def _():
            total = jnp.zeros((1, S), F32)
            place = scatter[:, : 2 * MSLOTS]
            for d in range(DOFS):
                delta = slots[: 2 * GY_N, d].reshape(2 * MSLOTS, S)
                high = delta.astype(BF16)
                low = (delta - high.astype(F32)).astype(BF16)
                total += finish(d, dot(place, high) + dot(place, low))
            squares[...] = total

    if not last:
        source = base if first else y
        for r in range(NB):
            rounded[r] = source[r * TILE : (r + 1) * TILE].astype(BF16)
        east[...] = rounded[NB - 1]
        west[...] = rounded[0]
        north[...] = rounded[1]
        south[...] = rounded[NB - 2]

        def collect(count):
            pick = gather[: count * MSLOTS]
            for d in range(DOFS):
                values = source[pl.ds(d, NODES, stride=DOFS), :].astype(BF16)
                rows = dot(pick, values)
                slots[: count * GY_N, d] = rows.reshape(count * GY_N, CAP, S)

        def message(q):
            return slots[q * GY_N : (q + 1) * GY_N].reshape(GY_N, ROWS_MSG, S).astype(BF16)

        @pl.when(is_rod)
        def _():
            collect(7)
            send_a[0] = jnp.zeros((GY_N, ROWS_MSG, S), BF16)
            send_b[0] = message(0)
            for q in range(3):
                send_a[q + 1] = message(q + 1)
                send_b[q + 1] = message(q + 4)

        @pl.when(jnp.logical_not(is_rod))
        def _():
            collect(1)
            send_a[0] = message(0)
            send_b[0] = message(0)
            for q in range(1, PAIRS):
                send_a[q] = jnp.zeros((GY_N, ROWS_MSG, S), BF16)
                send_b[q] = jnp.zeros((GY_N, ROWS_MSG, S), BF16)


def update(first, last, args):
    out = []
    if not last:
        out += [jax.ShapeDtypeStruct((NB, TILE, S), BF16)]
        out += [jax.ShapeDtypeStruct((TILE, S), BF16)] * 4
        out += [jax.ShapeDtypeStruct((PAIRS, GY_N, ROWS_MSG, S), BF16)] * 2
    else:
        out += [jax.ShapeDtypeStruct((ROWS, S), F32)]
    if not first:
        out += [jax.ShapeDtypeStruct((1, S), F32)]
    scratch = [pltpu.VMEM((7 * GY_N, DOFS, CAP, S), F32)]
    if not last:
        scratch += [pltpu.VMEM((ROWS, S), F32)]
    return pl.pallas_call(
        functools.partial(update_kernel, first, last),
        out_shape=out,
        in_specs=[SMEM] + [VMEM] * (len(args) - 1),
        out_specs=[VMEM] * len(out),
        scratch_shapes=scratch,
        compiler_params=pltpu.CompilerParams(vmem_limit_bytes=32 * 1024 * 1024),
        name="update",
    )(*args)


def product_kernel(columns, blocks, rounded, west, east, south, north, out, extended):
    r = pl.program_id(0)

    @pl.when(r == 0)
    def _():
        extended[:NB] = rounded[...]
        extended[NB] = west[...]
        extended[NB + 1] = east[...]
        extended[NB + 2] = south[...]
        extended[NB + 3] = north[...]

    total = dot(blocks[0, 0], extended[columns[r, 0]])
    for k in range(1, KB):
        total += dot(blocks[0, k], extended[columns[r, k]])
    out[...] = total


def product(columns, blocks, rounded, west, east, south, north):
    return pl.pallas_call(
        product_kernel,
        out_shape=jax.ShapeDtypeStruct((ROWS, S), F32),
        grid=(NB,),
        in_specs=[
            SMEM,
            pl.BlockSpec((1, KB, TILE, TILE), lambda r: (r, 0, 0, 0)),
            VMEM,
            VMEM,
            VMEM,
            VMEM,
            VMEM,
        ],
        out_specs=pl.BlockSpec((TILE, S), lambda r: (r, 0)),
        scratch_shapes=[pltpu.VMEM((NB + 4, TILE, S), BF16)],
        compiler_params=pltpu.CompilerParams(vmem_limit_bytes=32 * 1024 * 1024),
        cost_estimate=pl.CostEstimate(
            flops=2 * NB * KB * TILE * TILE * S, bytes_accessed=12_000_000, transcendentals=0
        ),
        name="product",
    )(columns, blocks, rounded, west, east, south, north)


def chain(count, step):
    return [(i, i + step) for i in range(count) if 0 <= i + step < count]


def halos(rounded_edges):
    (last, head, second, sixth) = rounded_edges
    west = lax.ppermute(last, "gx", chain(4, 1))
    east = lax.ppermute(head, "gx", chain(4, -1))
    south = lax.ppermute(second, GY, chain(8, 1))
    north = lax.ppermute(sixth, GY, chain(8, -1))
    return (west, east, south, north)


def norm_of(squares):
    spread = jnp.broadcast_to(squares, (256, S))
    gathered = lax.all_to_all(spread, EVERY, split_axis=0, concat_axis=0, tiled=True)
    return jnp.sqrt(jnp.sum(gathered, axis=0, keepdims=True) / ALL_DOFS + EPS)


def exchange(group, send_a, send_b):
    passed = lax.ppermute(send_b, GROUP, [(0, 1), (1, 0)])
    block = jnp.arange(PAIRS)
    relay = (group == 1) | ((group == 0) & (block == 0))
    send = jnp.where(relay[:, None, None, None], passed, send_a)
    received = lax.all_to_all(
        send.reshape(PAIRS * GY_N, ROWS_MSG, S),
        ("zh", "y", "zl"),
        split_axis=0,
        concat_axis=0,
        tiled=True,
    ).reshape(PAIRS, GY_N, ROWS_MSG, S)
    handed = lax.ppermute(received[1:], GROUP, [(1, 0)])
    return (received, handed)


def local(start_vectors, tile_blocks, block_columns, sleeve_rod, sleeve_membrane, sleeve_stiffness):
    group = lax.axis_index(GROUP)
    is_rod = group == 0
    memb = jnp.maximum(group - 1, 0)
    order = jnp.array(ORDER, jnp.int32)
    blocks = tile_blocks[0, 0, 0]
    columns = block_columns[0, 0, 0]

    rod_nodes = jnp.take(sleeve_rod[0, 0], order, axis=0).reshape(SLOTS)
    memb_nodes = lax.dynamic_index_in_dim(
        sleeve_membrane[0, :, :, 0, :], memb, axis=1, keepdims=False
    ).reshape(MSLOTS)
    memb_nodes = jnp.concatenate([memb_nodes, jnp.full((SLOTS - MSLOTS,), -1, jnp.int32)])
    nodes = jnp.where(is_rod, rod_nodes, memb_nodes)
    ids = jnp.arange(NODES, dtype=jnp.int32)
    gather = (nodes[:, None] == ids[None, :]).astype(BF16)
    scatter = (ids[:, None] == nodes[None, :]).astype(BF16)
    rod_flag = is_rod.astype(jnp.int32).reshape(1)

    start = start_vectors[0, 0, 0].reshape(ROWS, S)
    state = update(True, False, [rod_flag, start, gather])

    stiff = sleeve_stiffness[0, :, :, 0, :]
    rod_stiff = lax.all_to_all(
        stiff.reshape(GY_N, 7 * CAP), GY, split_axis=0, concat_axis=0, tiled=True
    ).reshape(GY_N, 7, CAP)
    rod_stiff = jnp.take(rod_stiff, order, axis=1).transpose(1, 0, 2).reshape(SLOTS)
    memb_stiff = lax.dynamic_index_in_dim(stiff, memb, axis=1, keepdims=False).reshape(MSLOTS)
    memb_stiff = jnp.concatenate([memb_stiff, jnp.zeros((SLOTS - MSLOTS,), F32)])
    kappa = jnp.where(is_rod, rod_stiff, memb_stiff)
    kappa = jnp.broadcast_to(kappa[:, None], (SLOTS, S))

    scales = []
    inverse = jnp.ones((1, S), F32)
    for turn in range(MATVECS):
        last = turn == MATVECS - 1
        (rounded, *edges) = state[:5]
        (send_a, send_b) = state[5:7]
        (recv_a, recv_b) = exchange(group, send_a, send_b)
        if turn:
            scales.append(norm_of(state[7]))
            inverse = 1.0 / scales[-1]
        base = product(columns, blocks, rounded, *halos(edges))
        args = [rod_flag, base, inverse, recv_a, recv_b, send_a, send_b, kappa, scatter]
        state = update(False, last, args + ([] if last else [gather]))
    (value, squares) = state
    scales.append(norm_of(squares))
    final = (value / scales[-1]).reshape(1, 1, 1, NB, TILE, S)
    return (final, jnp.concatenate(scales, axis=0))


def solution(mesh):
    fine = Mesh(mesh.devices.reshape(4, 2, 4, 4, 2), EVERY)
    spread = (GROUP, "gx", GY)
    return jax.shard_map(
        local,
        mesh=fine,
        in_specs=(
            P(*spread, None, None, None),
            P(*spread, None, None, None, None),
            P(*spread, None, None),
            P("gx", GY, None, None, None),
            P("gx", None, None, GY, None),
            P("gx", None, None, GY, None),
        ),
        out_specs=(P(*spread, None, None, None), P()),
        check_vma=False,
    )
```

time: 522 us -> 217 us (0.42); the launches traced: 512 us -> 215 us
  blocking collectives: 231 us -> 65.5 us
  waiting for transfers between devices: 90.3 us -> 7.48 us
  matrix products: 43.6 us -> 0 us
  local copies, waits for them, and re-layouts: 47.3 us -> 26.3 us
  Pallas kernels: 0 us -> 18.3 us
  other arithmetic: 22.9 us -> 8.02 us
  starting transfers between devices: 75 us -> 88.3 us
    psum x3 -> x0, blocking collectives: 231 us -> none  [local(): lax.psum(jnp.sum(coupled * coupled, axis=(0, 1)), ('group', 'gx', 'gy'))]
    all_to_all x0 -> x3, blocking collectives: none -> 65.5 us  [the longest x2 35.7 us: exchange(): lax.all_to_all(send.reshape(PAIRS * GY_N, ROWS_MSG, S), ('zh', 'y', 'zl')...]
    all_to_all x6 -> x4, waiting for transfers between devices: 66.3 us -> 4.4 us  [the longest x1 4.13 us: local(): lax.all_to_all(stiff.reshape(GY_N, 7 * CAP), GY, split_axis=0, concat_axi...]
    dot_general x9 -> x0, matrix products: 43.6 us -> none  [the longest x3 24.7 us: local(): jnp.einsum('rkij,rkjs->ris', blocks, picked, preferred_element_type=jnp.f...]
    ppermute x12 -> x18, starting transfers between devices: 28.6 us -> 52.6 us  [the longest x3 13.6 us: exchange(): passed = lax.ppermute(send_b, GROUP, [(0, 1), (1, 0)])]
    ppermute x12 -> x18, waiting for transfers between devices: 24.1 us -> 3.08 us  [the longest x3 1.73 us: exchange(): passed = lax.ppermute(send_b, GROUP, [(0, 1), (1, 0)])]
    pallas_call x0 -> x7, Pallas kernels: none -> 18.3 us  [the longest x3 13.7 us: product(): pl.pallas_call(product_kernel, out_shape=jax.ShapeDtypeStruct((ROWS, S),...]
    unnamed x23 -> x48, local copies, waits for them, and re-layouts: 2.77 us -> 19.6 us
  transfers between devices with their start and end apart: 18 -> 22, of which waited for: 10 -> 6; matrix products, arithmetic and copies ran while one was open for 7% -> 3% of each run, Pallas kernels for 0% -> 6%
where the time goes in v1:
time: 217 us; the launch traced here: 215 us
  starting transfers between devices  88.3 us (41%)
  blocking collectives  65.5 us (30%)
  local copies, waits for them, and re-layouts  26.3 us (12%)
  Pallas kernels  18.3 us (8%)
  other arithmetic  8.02 us (4%)
  waiting for transfers between devices  7.48 us (3%)
    all_to_all x2, blocking collectives, exchange(): lax.all_to_all(send.reshape(PAIRS * GY_N, ROWS_MSG, S), ('zh', 'y', 'zl')...  35.7 us
    all_to_all x1, blocking collectives, norm_of(): lax.all_to_all(spread, EVERY, split_axis=0, concat_axis=0, tiled=True)  29.8 us
    all_to_all x2, starting transfers between devices, norm_of(): lax.all_to_all(spread, EVERY, split_axis=0, concat_axis=0, tiled=True)  26.1 us
    unnamed x48, local copies, waits for them, and re-layouts  19.6 us
    pallas_call x3, Pallas kernels, product(): pl.pallas_call(product_kernel, out_shape=jax.ShapeDtypeStruct((ROWS, S),...  13.7 us
    ppermute x3, starting transfers between devices, exchange(): passed = lax.ppermute(send_b, GROUP, [(0, 1), (1, 0)])  13.6 us
    ppermute x3, starting transfers between devices, exchange(): handed = lax.ppermute(received[1:], GROUP, [(1, 0)])  12 us
    ppermute x3, starting transfers between devices, halos(): west = lax.ppermute(last, 'gx', chain(4, 1))  9.71 us
  transfers between devices with their start and end apart: 22, of which 6 were waited for; matrix products, arithmetic and copies ran while one was open for 3% of the time, Pallas kernels for 6%

profile of v1, /device:TPU:1, one launch (start us, length us, event | category | flops | bytes accessed | tf_op | source)
XLA Modules:
  0.0 215.1 jit_solution(3390200027010536935)
XLA Ops:
  2.9 1.4 copy-done.4
  5.5 5.7 %collective-permute-start.4 = (bf16[4,8,48,128]{3,2,1,0:T(8,128)(2,1)S(1)}, bf16[4,8,48,128]{3,2,1,0:T(8,128)(2,1)S(1)}, u32[]{:S(2)}, u32[]{:S(2)}) collective-permute-start(bf16[4,8,48,128]{3,2,1,0:T(8,128)(2,1)S(1)} %get-tuple-element.32.refs_6_), channel_id=1, source_target_pairs={{0,32},{32,0},{1,33},{33,1},{2,34},{34,2},{3,35},{35,3},{4,36},{36... | collective-permute-start | bytes 1179656 | tf_op jit(solution)/shard_map/ppermute | solution.py:229
  12.0 3.8 %all-to-all-start.1 = ((f32[8,1,56]{2,1,0:T(1,128)}), f32[8,1,56]{2,1,0:T(1,128)S(1)}, u32[]{:S(2)}, u32[]{:S(2)}) async-start(f32[8,1,56]{2,1,0:T(1,128)} %all_to_all.28), calls=%async_computation.1 | async-start | bytes 8192 | tf_op jit(solution)/shard_map/all_to_all | solution.py:267
  16.7 4.1 %all-to-all-done.1 = f32[8,1,56]{2,1,0:T(1,128)S(1)} async-done(((f32[8,1,56]{2,1,0:T(1,128)}), f32[8,1,56]{2,1,0:T(1,128)S(1)}, u32[]{:S(2)}, u32[]{:S(2)}) %all-to-all-start.1) | async-done | bytes 1824 | tf_op jit(solution)/shard_map/all_to_all | solution.py:267
  20.8 5.8 %all-to-all-start = ((bf16[32,48,128]{2,1,0:T(8,128)(2,1)}), bf16[32,48,128]{2,1,0:T(8,128)(2,1)S(1)}, u32[]{:S(2)}, u32[]{:S(2)}) async-start(bf16[32,48,128]{2,1,0:T(8,128)(2,1)} %bitcast.5), calls=%async_computation | async-start | bytes 786432 | tf_op jit(solution)/shard_map/all_to_all | solution.py:233
  26.6 3.1 %collective-permute-start = (bf16[384,128]{1,0:T(8,128)(2,1)}, bf16[384,128]{1,0:T(8,128)(2,1)S(1)}, u32[]{:S(2)}, u32[]{:S(2)}) collective-permute-start(bf16[384,128]{1,0:T(8,128)(2,1)} %get-tuple-element.28), channel_id=1, source_target_pairs={{0,8},{8,16},{16,24},{1,9},{9,17},{17,25},{2,10},{10,18},{18,26},{... | collective-permute-start | bytes 294920 | tf_op jit(solution)/shard_map/ppermute | solution.py:215
  29.7 1.3 collective-permute-start.1
  31.0 3.1 %collective-permute-start.2 = (bf16[384,128]{1,0:T(8,128)(2,1)}, bf16[384,128]{1,0:T(8,128)(2,1)S(1)}, u32[]{:S(2)}, u32[]{:S(2)}) collective-permute-start(bf16[384,128]{1,0:T(8,128)(2,1)} %get-tuple-element.30), channel_id=1, source_target_pairs={{0,1},{1,2},{2,3},{3,4},{4,5},{5,6},{6,7},{8,9},{9,10},{10,11},{11... | collective-permute-start | bytes 294920 | tf_op jit(solution)/shard_map/ppermute | solution.py:217
  34.2 1.3 collective-permute-start.3
  38.1 6.3 %collective-permute-start.5 = (bf16[3,8,48,128]{3,2,1,0:T(8,128)(2,1)S(1)}, bf16[3,8,48,128]{3,2,1,0:T(8,128)(2,1)S(1)}, u32[]{:S(2)}, u32[]{:S(2)}) collective-permute-start(bf16[3,8,48,128]{3,2,1,0:T(8,128)(2,1)S(1)} %bitcast.46), channel_id=1, source_target_pairs={{32,0},{33,1},{34,2},{35,3},{36,4},{37,5},{38,6},{39,7},{40,8},{41... | collective-permute-start | bytes 884744 | tf_op jit(solution)/shard_map/ppermute | solution.py:240
  44.5 3.7 %copy-done.1 = bf16[1,1,1,8,4,384,384]{6,5,4,3,2,1,0:T(8,128)(2,1)S(1)} copy-done((bf16[1,1,1,8,4,384,384]{6,5,4,3,2,1,0:T(8,128)(2,1)S(1)}, bf16[1,1,1,8,4,384,384]{6,5,4,3,2,1,0:T(8,128)(2,1)}, u32[]{:S(2)}) %copy-start.1) | copy-done | bytes 9437208
  48.2 4.6 %product.3.refs_1_ = f32[3072,128]{1,0:T(8,128)S(1)} custom-call(s32[8,4]{1,0:T(8,128)S(1)} %copy.28.columns, bf16[8,4,384,384]{3,2,1,0:T(8,128)(2,1)S(1)} %bitcast.32, bf16[8,384,128]{2,1,0:T(8,128)(2,1)S(1)} %get-tuple-element.27.rounded, bf16[384,128]{1,0:T(8,128)(2,1)S(1)} %collective-permute-done.west, ...), custom_call_target="tpu_custom_call" | custom-call | flops 1207959552 | bytes 12000000 | tf_op jit(solution)/shard_map/product/pallas_call | solution.py:186
  52.9 1.8 update.5
  54.7 2.5 %collective-permute-start.10 = (bf16[4,8,48,128]{3,2,1,0:T(8,128)(2,1)S(1)}, bf16[4,8,48,128]{3,2,1,0:T(8,128)(2,1)S(1)}, u32[]{:S(2)}, u32[]{:S(2)}) collective-permute-start(bf16[4,8,48,128]{3,2,1,0:T(8,128)(2,1)S(1)} %get-tuple-element.40.refs_6_), channel_id=1, source_target_pairs={{0,32},{32,0},{1,33},{33,1},{2,34},{34,2},{3,35},{35,3},{4,36},{36... | collective-permute-start | bytes 1179656 | tf_op jit(solution)/shard_map/ppermute | solution.py:229
  58.6 18.4 %all_to_all.42 = bf16[32,48,128]{2,1,0:T(8,128)(2,1)S(1)} all-to-all(bf16[32,48,128]{2,1,0:T(8,128)(2,1)S(1)} %bitcast.43), channel_id=1, replica_groups=mesh['zh'=4,'core'=2,'gx'=4,'y'=4,'zl'=2] {'zh','y','zl'}, dimensions={0} | all-to-all | bytes 786432 | tf_op jit(solution)/shard_map/all_to_all | solution.py:233
  77.8 12.5 %all-to-all-start.2 = ((f32[256,1,128]{2,1,0:T(1,128)}), f32[256,1,128]{2,1,0:T(1,128)}, u32[]{:S(2)}, u32[]{:S(2)}) async-start(f32[256,1,128]{2,1,0:T(1,128)} %broadcast_in_dim.76), calls=%async_computation.2 | async-start | bytes 262144 | tf_op jit(solution)/shard_map/all_to_all | solution.py:224
  90.3 3.3 %collective-permute-start.6 = (bf16[384,128]{1,0:T(8,128)(2,1)}, bf16[384,128]{1,0:T(8,128)(2,1)S(1)}, u32[]{:S(2)}, u32[]{:S(2)}) collective-permute-start(bf16[384,128]{1,0:T(8,128)(2,1)} %get-tuple-element.35), channel_id=1, source_target_pairs={{0,8},{8,16},{16,24},{1,9},{9,17},{17,25},{2,10},{10,18},{18,26},{... | collective-permute-start | bytes 294920 | tf_op jit(solution)/shard_map/ppermute | solution.py:215
  93.6 1.3 collective-permute-start.7
  94.9 3.2 %collective-permute-start.8 = (bf16[384,128]{1,0:T(8,128)(2,1)}, bf16[384,128]{1,0:T(8,128)(2,1)S(1)}, u32[]{:S(2)}, u32[]{:S(2)}) collective-permute-start(bf16[384,128]{1,0:T(8,128)(2,1)} %get-tuple-element.37), channel_id=1, source_target_pairs={{0,1},{1,2},{2,3},{3,4},{4,5},{5,6},{6,7},{8,9},{9,10},{10,11},{11... | collective-permute-start | bytes 294920 | tf_op jit(solution)/shard_map/ppermute | solution.py:217
  100.2 2.8 %collective-permute-start.11 = (bf16[3,8,48,128]{3,2,1,0:T(8,128)(2,1)}, bf16[3,8,48,128]{3,2,1,0:T(8,128)(2,1)S(1)}, u32[]{:S(2)}, u32[]{:S(2)}) collective-permute-start(bf16[3,8,48,128]{3,2,1,0:T(8,128)(2,1)} %bitcast.13), channel_id=1, source_target_pairs={{32,0},{33,1},{34,2},{35,3},{36,4},{37,5},{38,6},{39,7},{40,8},{41... | collective-permute-start | bytes 884744 | tf_op jit(solution)/shard_map/ppermute | solution.py:240
  103.7 3.7 %copy-done.2 = bf16[1,1,1,8,4,384,384]{6,5,4,3,2,1,0:T(8,128)(2,1)S(1)} copy-done((bf16[1,1,1,8,4,384,384]{6,5,4,3,2,1,0:T(8,128)(2,1)S(1)}, bf16[1,1,1,8,4,384,384]{6,5,4,3,2,1,0:T(8,128)(2,1)}, u32[]{:S(2)}) %copy-start.2) | copy-done | bytes 9437208
  108.5 4.6 %product.4.refs_1_ = f32[3072,128]{1,0:T(8,128)S(1)} custom-call(s32[8,4]{1,0:T(8,128)S(1)} %copy.28.columns, bf16[8,4,384,384]{3,2,1,0:T(8,128)(2,1)S(1)} %bitcast.33, bf16[8,384,128]{2,1,0:T(8,128)(2,1)S(1)} %copy-done.13, bf16[384,128]{1,0:T(8,128)(2,1)S(1)} %collective-permute-done.6.west, bf16[384,128]{1,0:T(8,128)(2,1)S(1)} %collective-permute-done.7.east, ...), custom_call_target="tpu_custom_call" | custom-call | flops 1207959552 | bytes 12000000 | tf_op jit(solution)/shard_map/product/pallas_call | solution.py:186
  117.2 5.3 %collective-permute-start.16 = (bf16[4,8,48,128]{3,2,1,0:T(8,128)(2,1)S(1)}, bf16[4,8,48,128]{3,2,1,0:T(8,128)(2,1)S(1)}, u32[]{:S(2)}, u32[]{:S(2)}) collective-permute-start(bf16[4,8,48,128]{3,2,1,0:T(8,128)(2,1)S(1)} %get-tuple-element.48.refs_6_), channel_id=1, source_target_pairs={{0,32},{32,0},{1,33},{33,1},{2,34},{34,2},{3,35},{35,3},{4,36},{36... | collective-permute-start | bytes 1179656 | tf_op jit(solution)/shard_map/ppermute | solution.py:229
  123.8 17.3 %all_to_all.43 = bf16[32,48,128]{2,1,0:T(8,128)(2,1)S(1)} all-to-all(bf16[32,48,128]{2,1,0:T(8,128)(2,1)S(1)} %bitcast.42), channel_id=1, replica_groups=mesh['zh'=4,'core'=2,'gx'=4,'y'=4,'zl'=2] {'zh','y','zl'}, dimensions={0} | all-to-all | bytes 786432 | tf_op jit(solution)/shard_map/all_to_all | solution.py:233
  141.8 13.6 %all-to-all-start.4 = ((f32[256,1,128]{2,1,0:T(1,128)}), f32[256,1,128]{2,1,0:T(1,128)}, u32[]{:S(2)}, u32[]{:S(2)}) async-start(f32[256,1,128]{2,1,0:T(1,128)} %broadcast_in_dim.77), calls=%async_computation.4 | async-start | bytes 262144 | tf_op jit(solution)/shard_map/all_to_all | solution.py:224
  155.4 3.3 %collective-permute-start.12 = (bf16[384,128]{1,0:T(8,128)(2,1)}, bf16[384,128]{1,0:T(8,128)(2,1)S(1)}, u32[]{:S(2)}, u32[]{:S(2)}) collective-permute-start(bf16[384,128]{1,0:T(8,128)(2,1)} %copy-done.21), channel_id=1, source_target_pairs={{0,8},{8,16},{16,24},{1,9},{9,17},{17,25},{2,10},{10,18},{18,26},{... | collective-permute-start | bytes 294920 | tf_op jit(solution)/shard_map/ppermute | solution.py:215
  160.0 3.2 %collective-permute-start.14 = (bf16[384,128]{1,0:T(8,128)(2,1)}, bf16[384,128]{1,0:T(8,128)(2,1)S(1)}, u32[]{:S(2)}, u32[]{:S(2)}) collective-permute-start(bf16[384,128]{1,0:T(8,128)(2,1)} %copy-done.19), channel_id=1, source_target_pairs={{0,1},{1,2},{2,3},{3,4},{4,5},{5,6},{6,7},{8,9},{9,10},{10,11},{11... | collective-permute-start | bytes 294920 | tf_op jit(solution)/shard_map/ppermute | solution.py:217
  165.3 2.8 %collective-permute-start.17 = (bf16[3,8,48,128]{3,2,1,0:T(8,128)(2,1)}, bf16[3,8,48,128]{3,2,1,0:T(8,128)(2,1)S(1)}, u32[]{:S(2)}, u32[]{:S(2)}) collective-permute-start(bf16[3,8,48,128]{3,2,1,0:T(8,128)(2,1)} %bitcast.19), channel_id=1, source_target_pairs={{32,0},{33,1},{34,2},{35,3},{36,4},{37,5},{38,6},{39,7},{40,8},{41... | collective-permute-start | bytes 884744 | tf_op jit(solution)/shard_map/ppermute | solution.py:240
  168.8 3.7 %copy-done.3 = bf16[1,1,1,8,4,384,384]{6,5,4,3,2,1,0:T(8,128)(2,1)S(1)} copy-done((bf16[1,1,1,8,4,384,384]{6,5,4,3,2,1,0:T(8,128)(2,1)S(1)}, bf16[1,1,1,8,4,384,384]{6,5,4,3,2,1,0:T(8,128)(2,1)}, u32[]{:S(2)}) %copy-start.3) | copy-done | bytes 9437208
  173.6 4.6 %product.5.refs_1_ = f32[3072,128]{1,0:T(8,128)S(1)} custom-call(s32[8,4]{1,0:T(8,128)S(1)} %copy.28.columns, bf16[8,4,384,384]{3,2,1,0:T(8,128)(2,1)S(1)} %bitcast.34, bf16[8,384,128]{2,1,0:T(8,128)(2,1)S(1)} %copy-done.11, bf16[384,128]{1,0:T(8,128)(2,1)S(1)} %collective-permute-done.12.west, bf16[384,128]{1,0:T(8,128)(2,1)S(1)} %collective-permute-done.13.east, ...), custom_call_target="tpu_custom_call" | custom-call | flops 1207959552 | bytes 12000000 | tf_op jit(solution)/shard_map/product/pallas_call | solution.py:186
  182.0 29.8 %all_to_all.44 = f32[256,1,128]{2,1,0:T(1,128)S(1)} all-to-all(f32[256,1,128]{2,1,0:T(1,128)S(1)} %broadcast_in_dim.78), channel_id=1, replica_groups=mesh['zh'=4,'core'=2,'gx'=4,'y'=4,'zl'=2] {'zh','core','gx','y','zl'}, dimensions={0} | all-to-all | bytes 262144 | tf_op jit(solution)/shard_map/all_to_all | solution.py:224
  211.9 2.7 %broadcast_divide_fusion = f32[3072,128]{1,0:T(8,128)} fusion(f32[3072,128]{1,0:T(8,128)} %copy-done.9, f32[128]{0:T(128)S(1)} %get-tuple-element.57), kind=kLoop, calls=%fused_computation.6 | loop fusion | flops 393216 | bytes 3146240 | tf_op jit(solution)/shard_map/div | solution.py:291
  (110 shorter events, 29.2 us)
Async XLA Ops:
  0.6 10.6 %copy-start.22 = (f32[1,8,7,1,8]{4,3,2,1,0:T(1,128)S(1)}, f32[1,8,7,1,8]{4,3,2,1,0:T(1,128)}, u32[]{:S(2)}) copy-start(f32[1,8,7,1,8]{4,3,2,1,0:T(1,128)} %param.12) | copy-start | bytes 5380
  4.3 31.1 %copy-start.23 = (s32[1,1,1,8,4]{3,4,2,1,0:T(4,128)S(1)}, s32[1,1,1,8,4]{3,4,2,1,0:T(4,128)}, u32[]{:S(2)}) copy-start(s32[1,1,1,8,4]{3,4,2,1,0:T(4,128)} %param.9) | copy-start | bytes 388
  5.5 10.3 %collective-permute-start.4 = (bf16[4,8,48,128]{3,2,1,0:T(8,128)(2,1)S(1)}, bf16[4,8,48,128]{3,2,1,0:T(8,128)(2,1)S(1)}, u32[]{:S(2)}, u32[]{:S(2)}) collective-permute-start(bf16[4,8,48,128]{3,2,1,0:T(8,128)(2,1)S(1)} %get-tuple-element.32.refs_6_), channel_id=1, source_target_pairs={{0,32},{32,0},{1,33},{33,1},{2,34},{34,2},{3,35},{35,3},{4,36},{36... | collective-permute-start | bytes 1179656 | tf_op jit(solution)/shard_map/ppermute | solution.py:229
  12.0 8.8 %all-to-all-start.1 = ((f32[8,1,56]{2,1,0:T(1,128)}), f32[8,1,56]{2,1,0:T(1,128)S(1)}, u32[]{:S(2)}, u32[]{:S(2)}) async-start(f32[8,1,56]{2,1,0:T(1,128)} %all_to_all.28), calls=%async_computation.1 | async-start | bytes 8192 | tf_op jit(solution)/shard_map/all_to_all | solution.py:267
  20.8 17.3 %all-to-all-start = ((bf16[32,48,128]{2,1,0:T(8,128)(2,1)}), bf16[32,48,128]{2,1,0:T(8,128)(2,1)S(1)}, u32[]{:S(2)}, u32[]{:S(2)}) async-start(bf16[32,48,128]{2,1,0:T(8,128)(2,1)} %bitcast.5), calls=%async_computation | async-start | bytes 786432 | tf_op jit(solution)/shard_map/all_to_all | solution.py:233
  26.6 17.9 %collective-permute-start = (bf16[384,128]{1,0:T(8,128)(2,1)}, bf16[384,128]{1,0:T(8,128)(2,1)S(1)}, u32[]{:S(2)}, u32[]{:S(2)}) collective-permute-start(bf16[384,128]{1,0:T(8,128)(2,1)} %get-tuple-element.28), channel_id=1, source_target_pairs={{0,8},{8,16},{16,24},{1,9},{9,17},{17,25},{2,10},{10,18},{18,26},{... | collective-permute-start | bytes 294920 | tf_op jit(solution)/shard_map/ppermute | solution.py:215
  29.7 14.7 %collective-permute-start.1 = (bf16[384,128]{1,0:T(8,128)(2,1)}, bf16[384,128]{1,0:T(8,128)(2,1)S(1)}, u32[]{:S(2)}, u32[]{:S(2)}) collective-permute-start(bf16[384,128]{1,0:T(8,128)(2,1)} %get-tuple-element.29), channel_id=1, source_target_pairs={{8,0},{16,8},{24,16},{9,1},{17,9},{25,17},{10,2},{18,10},{26,18},{... | collective-permute-start | bytes 294920 | tf_op jit(solution)/shard_map/ppermute | solution.py:216
  31.0 13.5 %collective-permute-start.2 = (bf16[384,128]{1,0:T(8,128)(2,1)}, bf16[384,128]{1,0:T(8,128)(2,1)S(1)}, u32[]{:S(2)}, u32[]{:S(2)}) collective-permute-start(bf16[384,128]{1,0:T(8,128)(2,1)} %get-tuple-element.30), channel_id=1, source_target_pairs={{0,1},{1,2},{2,3},{3,4},{4,5},{5,6},{6,7},{8,9},{9,10},{10,11},{11... | collective-permute-start | bytes 294920 | tf_op jit(solution)/shard_map/ppermute | solution.py:217
  34.2 10.3 %collective-permute-start.3 = (bf16[384,128]{1,0:T(8,128)(2,1)S(1)}, bf16[384,128]{1,0:T(8,128)(2,1)S(1)}, u32[]{:S(2)}, u32[]{:S(2)}) collective-permute-start(bf16[384,128]{1,0:T(8,128)(2,1)S(1)} %get-tuple-element.31), channel_id=1, source_target_pairs={{1,0},{2,1},{3,2},{4,3},{5,4},{6,5},{7,6},{9,8},{10,9},{11,10},{12... | collective-permute-start | bytes 294920 | tf_op jit(solution)/shard_map/ppermute | solution.py:218
  38.1 14.7 %collective-permute-start.5 = (bf16[3,8,48,128]{3,2,1,0:T(8,128)(2,1)S(1)}, bf16[3,8,48,128]{3,2,1,0:T(8,128)(2,1)S(1)}, u32[]{:S(2)}, u32[]{:S(2)}) collective-permute-start(bf16[3,8,48,128]{3,2,1,0:T(8,128)(2,1)S(1)} %bitcast.46), channel_id=1, source_target_pairs={{32,0},{33,1},{34,2},{35,3},{36,4},{37,5},{38,6},{39,7},{40,8},{41... | collective-permute-start | bytes 884744 | tf_op jit(solution)/shard_map/ppermute | solution.py:240
  54.7 49.0 %copy-start.12 = (bf16[8,384,128]{2,1,0:T(8,128)(2,1)}, bf16[8,384,128]{2,1,0:T(8,128)(2,1)S(1)}, u32[]{:S(2)}) copy-start(bf16[8,384,128]{2,1,0:T(8,128)(2,1)S(1)} %get-tuple-element.34.rounded) | copy-start | bytes 2359300
  54.7 3.8 %collective-permute-start.10 = (bf16[4,8,48,128]{3,2,1,0:T(8,128)(2,1)S(1)}, bf16[4,8,48,128]{3,2,1,0:T(8,128)(2,1)S(1)}, u32[]{:S(2)}, u32[]{:S(2)}) collective-permute-start(bf16[4,8,48,128]{3,2,1,0:T(8,128)(2,1)S(1)} %get-tuple-element.40.refs_6_), channel_id=1, source_target_pairs={{0,32},{32,0},{1,33},{33,1},{2,34},{34,2},{3,35},{35,3},{4,36},{36... | collective-permute-start | bytes 1179656 | tf_op jit(solution)/shard_map/ppermute | solution.py:229
  77.8 35.3 %all-to-all-start.2 = ((f32[256,1,128]{2,1,0:T(1,128)}), f32[256,1,128]{2,1,0:T(1,128)}, u32[]{:S(2)}, u32[]{:S(2)}) async-start(f32[256,1,128]{2,1,0:T(1,128)} %broadcast_in_dim.76), calls=%async_computation.2 | async-start | bytes 262144 | tf_op jit(solution)/shard_map/all_to_all | solution.py:224
  90.3 12.7 %collective-permute-start.6 = (bf16[384,128]{1,0:T(8,128)(2,1)}, bf16[384,128]{1,0:T(8,128)(2,1)S(1)}, u32[]{:S(2)}, u32[]{:S(2)}) collective-permute-start(bf16[384,128]{1,0:T(8,128)(2,1)} %get-tuple-element.35), channel_id=1, source_target_pairs={{0,8},{8,16},{16,24},{1,9},{9,17},{17,25},{2,10},{10,18},{18,26},{... | collective-permute-start | bytes 294920 | tf_op jit(solution)/shard_map/ppermute | solution.py:215
  93.6 9.4 %collective-permute-start.7 = (bf16[384,128]{1,0:T(8,128)(2,1)}, bf16[384,128]{1,0:T(8,128)(2,1)S(1)}, u32[]{:S(2)}, u32[]{:S(2)}) collective-permute-start(bf16[384,128]{1,0:T(8,128)(2,1)} %get-tuple-element.36), channel_id=1, source_target_pairs={{8,0},{16,8},{24,16},{9,1},{17,9},{25,17},{10,2},{18,10},{26,18},{... | collective-permute-start | bytes 294920 | tf_op jit(solution)/shard_map/ppermute | solution.py:216
  94.9 8.1 %collective-permute-start.8 = (bf16[384,128]{1,0:T(8,128)(2,1)}, bf16[384,128]{1,0:T(8,128)(2,1)S(1)}, u32[]{:S(2)}, u32[]{:S(2)}) collective-permute-start(bf16[384,128]{1,0:T(8,128)(2,1)} %get-tuple-element.37), channel_id=1, source_target_pairs={{0,1},{1,2},{2,3},{3,4},{4,5},{5,6},{6,7},{8,9},{9,10},{10,11},{11... | collective-permute-start | bytes 294920 | tf_op jit(solution)/shard_map/ppermute | solution.py:217
  98.1 5.6 %collective-permute-start.9 = (bf16[384,128]{1,0:T(8,128)(2,1)}, bf16[384,128]{1,0:T(8,128)(2,1)S(1)}, u32[]{:S(2)}, u32[]{:S(2)}) collective-permute-start(bf16[384,128]{1,0:T(8,128)(2,1)} %get-tuple-element.38), channel_id=1, source_target_pairs={{1,0},{2,1},{3,2},{4,3},{5,4},{6,5},{7,6},{9,8},{10,9},{11,10},{12... | collective-permute-start | bytes 294920 | tf_op jit(solution)/shard_map/ppermute | solution.py:218
  100.2 13.9 %collective-permute-start.11 = (bf16[3,8,48,128]{3,2,1,0:T(8,128)(2,1)}, bf16[3,8,48,128]{3,2,1,0:T(8,128)(2,1)S(1)}, u32[]{:S(2)}, u32[]{:S(2)}) collective-permute-start(bf16[3,8,48,128]{3,2,1,0:T(8,128)(2,1)} %bitcast.13), channel_id=1, source_target_pairs={{32,0},{33,1},{34,2},{35,3},{36,4},{37,5},{38,6},{39,7},{40,8},{41... | collective-permute-start | bytes 884744 | tf_op jit(solution)/shard_map/ppermute | solution.py:240
  117.1 6.7 %copy-start.7 = (bf16[4,8,48,128]{3,2,1,0:T(8,128)(2,1)}, bf16[4,8,48,128]{3,2,1,0:T(8,128)(2,1)S(1)}, u32[]{:S(2)}) copy-start(bf16[4,8,48,128]{3,2,1,0:T(8,128)(2,1)S(1)} %get-tuple-element.49.refs_5_) | copy-start | bytes 1179652
  117.1 6.7 %copy-start.10 = (bf16[8,384,128]{2,1,0:T(8,128)(2,1)}, bf16[8,384,128]{2,1,0:T(8,128)(2,1)S(1)}, u32[]{:S(2)}) copy-start(bf16[8,384,128]{2,1,0:T(8,128)(2,1)S(1)} %get-tuple-element.42.rounded) | copy-start | bytes 2359300
  117.1 23.9 %copy-start.16 = (bf16[4,8,48,128]{3,2,1,0:T(8,128)(2,1)}, bf16[4,8,48,128]{3,2,1,0:T(8,128)(2,1)S(1)}, u32[]{:S(2)}) copy-start(bf16[4,8,48,128]{3,2,1,0:T(8,128)(2,1)S(1)} %get-tuple-element.48.refs_6_) | copy-start | bytes 1179652
  117.1 23.9 %copy-start.18 = (bf16[384,128]{1,0:T(8,128)(2,1)}, bf16[384,128]{1,0:T(8,128)(2,1)S(1)}, u32[]{:S(2)}) copy-start(bf16[384,128]{1,0:T(8,128)(2,1)S(1)} %get-tuple-element.46) | copy-start | bytes 294916
  117.1 23.9 %copy-start.19 = (bf16[384,128]{1,0:T(8,128)(2,1)}, bf16[384,128]{1,0:T(8,128)(2,1)S(1)}, u32[]{:S(2)}) copy-start(bf16[384,128]{1,0:T(8,128)(2,1)S(1)} %get-tuple-element.45) | copy-start | bytes 294916
  117.1 23.9 %copy-start.20 = (bf16[384,128]{1,0:T(8,128)(2,1)}, bf16[384,128]{1,0:T(8,128)(2,1)S(1)}, u32[]{:S(2)}) copy-start(bf16[384,128]{1,0:T(8,128)(2,1)S(1)} %get-tuple-element.44) | copy-start | bytes 294916
  117.1 23.9 %copy-start.21 = (bf16[384,128]{1,0:T(8,128)(2,1)}, bf16[384,128]{1,0:T(8,128)(2,1)S(1)}, u32[]{:S(2)}) copy-start(bf16[384,128]{1,0:T(8,128)(2,1)S(1)} %get-tuple-element.43) | copy-start | bytes 294916
  117.2 6.5 %collective-permute-start.16 = (bf16[4,8,48,128]{3,2,1,0:T(8,128)(2,1)S(1)}, bf16[4,8,48,128]{3,2,1,0:T(8,128)(2,1)S(1)}, u32[]{:S(2)}, u32[]{:S(2)}) collective-permute-start(bf16[4,8,48,128]{3,2,1,0:T(8,128)(2,1)S(1)} %get-tuple-element.48.refs_6_), channel_id=1, source_target_pairs={{0,32},{32,0},{1,33},{33,1},{2,34},{34,2},{3,35},{35,3},{4,36},{36... | collective-permute-start | bytes 1179656 | tf_op jit(solution)/shard_map/ppermute | solution.py:229
  141.8 36.4 %all-to-all-start.4 = ((f32[256,1,128]{2,1,0:T(1,128)}), f32[256,1,128]{2,1,0:T(1,128)}, u32[]{:S(2)}, u32[]{:S(2)}) async-start(f32[256,1,128]{2,1,0:T(1,128)} %broadcast_in_dim.77), calls=%async_computation.4 | async-start | bytes 262144 | tf_op jit(solution)/shard_map/all_to_all | solution.py:224
  155.4 12.7 %collective-permute-start.12 = (bf16[384,128]{1,0:T(8,128)(2,1)}, bf16[384,128]{1,0:T(8,128)(2,1)S(1)}, u32[]{:S(2)}, u32[]{:S(2)}) collective-permute-start(bf16[384,128]{1,0:T(8,128)(2,1)} %copy-done.21), channel_id=1, source_target_pairs={{0,8},{8,16},{16,24},{1,9},{9,17},{17,25},{2,10},{10,18},{18,26},{... | collective-permute-start | bytes 294920 | tf_op jit(solution)/shard_map/ppermute | solution.py:215
  158.7 9.4 %collective-permute-start.13 = (bf16[384,128]{1,0:T(8,128)(2,1)}, bf16[384,128]{1,0:T(8,128)(2,1)S(1)}, u32[]{:S(2)}, u32[]{:S(2)}) collective-permute-start(bf16[384,128]{1,0:T(8,128)(2,1)} %copy-done.20), channel_id=1, source_target_pairs={{8,0},{16,8},{24,16},{9,1},{17,9},{25,17},{10,2},{18,10},{26,18},{... | collective-permute-start | bytes 294920 | tf_op jit(solution)/shard_map/ppermute | solution.py:216
  160.0 8.1 %collective-permute-start.14 = (bf16[384,128]{1,0:T(8,128)(2,1)}, bf16[384,128]{1,0:T(8,128)(2,1)S(1)}, u32[]{:S(2)}, u32[]{:S(2)}) collective-permute-start(bf16[384,128]{1,0:T(8,128)(2,1)} %copy-done.19), channel_id=1, source_target_pairs={{0,1},{1,2},{2,3},{3,4},{4,5},{5,6},{6,7},{8,9},{9,10},{10,11},{11... | collective-permute-start | bytes 294920 | tf_op jit(solution)/shard_map/ppermute | solution.py:217
  163.2 5.6 %collective-permute-start.15 = (bf16[384,128]{1,0:T(8,128)(2,1)}, bf16[384,128]{1,0:T(8,128)(2,1)S(1)}, u32[]{:S(2)}, u32[]{:S(2)}) collective-permute-start(bf16[384,128]{1,0:T(8,128)(2,1)} %copy-done.18), channel_id=1, source_target_pairs={{1,0},{2,1},{3,2},{4,3},{5,4},{6,5},{7,6},{9,8},{10,9},{11,10},{12... | collective-permute-start | bytes 294920 | tf_op jit(solution)/shard_map/ppermute | solution.py:218
  165.3 13.9 %collective-permute-start.17 = (bf16[3,8,48,128]{3,2,1,0:T(8,128)(2,1)}, bf16[3,8,48,128]{3,2,1,0:T(8,128)(2,1)S(1)}, u32[]{:S(2)}, u32[]{:S(2)}) collective-permute-start(bf16[3,8,48,128]{3,2,1,0:T(8,128)(2,1)} %bitcast.19), channel_id=1, source_target_pairs={{32,0},{33,1},{34,2},{35,3},{36,4},{37,5},{38,6},{39,7},{40,8},{41... | collective-permute-start | bytes 884744 | tf_op jit(solution)/shard_map/ppermute | solution.py:240
  (14 other events, 30.6 us)

commit v2 on v1

v2 whole, which is shorter than its diff:
```python
import functools

import jax
import jax.numpy as jnp
from jax import lax
from jax.experimental import pallas as pl
from jax.experimental.pallas import tpu as pltpu
from jax.sharding import PartitionSpec as P

MATVECS = 3
TILE = 384
NB = 8
KB = 4
S = 128
CAP = 8
DOFS = 6
NODES = NB * TILE // DOFS
ROWS = NB * TILE
GROUPS = 8
MEMB = GROUPS - 1
GX_N = 4
GY_N = 8
DEVICES = GROUPS * GX_N * GY_N
SLOTS = MEMB * GY_N * CAP
MSLOTS = GY_N * CAP
MESSAGE = DOFS * CAP
EPS = 1e-06
ALL_DOFS = DEVICES * ROWS
LOWEST, HIGHEST = 1e-20, 1e20

EVERY = ("group", "gx", "gy")

VMEM = pl.BlockSpec(memory_space=pltpu.VMEM)
SMEM = pl.BlockSpec(memory_space=pltpu.SMEM)
BF16 = jnp.bfloat16
F32 = jnp.float32


def dot(a, b):
    return jnp.dot(a, b, preferred_element_type=F32)


def update_kernel(turn, scaled, *refs):
    refs = list(refs)
    take = lambda n: [refs.pop(0) for _ in range(n)]
    first, last = turn == 0, turn == MATVECS
    (rod, base) = take(2)
    if first:
        (stiff_message, gather) = take(2)
    else:
        (received, own, kappa_in, scatter) = take(4)
        if not last:
            (gather,) = take(1)
        if scaled:
            (inverse,) = take(1)
    if last:
        (y,) = take(1)
    else:
        (rounded, east, west, north, south, send) = take(6)
    if not first:
        (squares,) = take(1)
    kappa = None
    if turn == 1:
        (kappa,) = take(1)
    elif not first:
        kappa = kappa_in
    (slots,) = take(1)
    if not first and not last:
        (y,) = take(1)
    is_rod = rod[0] == 1

    def on_rod(f):
        pl.when(is_rod)(f)

    def on_membrane(f):
        pl.when(jnp.logical_not(is_rod))(f)

    if not first:

        def difference(q, block):
            gap = own[block].astype(F32) - received[block].astype(F32)
            stiff = kappa[q * MSLOTS : (q + 1) * MSLOTS].reshape(GY_N, 1, CAP, S)
            slots[q * GY_N : (q + 1) * GY_N] = gap.reshape(GY_N, DOFS, CAP, S) * stiff

        @on_rod
        def _():
            if turn == 1:
                parts = received[0].astype(F32)
                lane = lax.broadcasted_iota(jnp.int32, parts.shape, 2)
                low = jnp.sum(jnp.where(lane < 3, parts, 0.0), axis=2, keepdims=True)
                high = jnp.sum(
                    jnp.where((lane >= 3) & (lane < 6), parts, 0.0)[:, :CAP], axis=2, keepdims=True
                )
                for m in range(MEMB):
                    value = low[:, m * CAP : (m + 1) * CAP] if m < DOFS else high
                    kappa[m * MSLOTS : (m + 1) * MSLOTS] = jnp.broadcast_to(
                        value, (GY_N, CAP, S)
                    ).reshape(MSLOTS, S)
            for q in range(MEMB):
                difference(q, q + 1)

        @on_membrane
        def _():
            if turn == 1:
                kappa[...] = kappa_in[...]
            difference(0, 0)
            slots[GY_N : 2 * GY_N] = jnp.zeros((GY_N, DOFS, CAP, S), F32)

        def finish(d, coupling):
            value = base[pl.ds(d, NODES, stride=DOFS), :] + coupling
            if scaled:
                value = value * inverse[...]
            y[pl.ds(d, NODES, stride=DOFS), :] = value
            part = jnp.sum(jnp.square(value).reshape(NODES // 8, 8, S), axis=0)
            return jnp.sum(part, axis=0, keepdims=True)

        @on_rod
        def _():
            total = jnp.zeros((1, S), F32)
            for d in range(DOFS):
                delta = slots[:, d].reshape(SLOTS, S)
                total += finish(d, dot(scatter[...], delta.astype(BF16)))
            squares[...] = total

        @on_membrane
        def _():
            total = jnp.zeros((1, S), F32)
            place = scatter[:, : 2 * MSLOTS]
            for d in range(DOFS):
                delta = slots[: 2 * GY_N, d].reshape(2 * MSLOTS, S)
                high = delta.astype(BF16)
                low = (delta - high.astype(F32)).astype(BF16)
                total += finish(d, dot(place, high) + dot(place, low))
            squares[...] = total

    if not last:
        source = base if first else y

        def collect(count):
            pick = gather[: count * MSLOTS]
            for d in range(DOFS):
                values = source[pl.ds(d, NODES, stride=DOFS), :].astype(BF16)
                rows = dot(pick, values)
                slots[: count * GY_N, d] = rows.reshape(count * GY_N, CAP, S)

        def message(q):
            return slots[q * GY_N : (q + 1) * GY_N].reshape(GY_N, MESSAGE, S).astype(BF16)

        @on_rod
        def _():
            collect(MEMB)
            if first:
                send[0] = stiff_message[...]
            for q in range(MEMB):
                send[q + 1] = message(q)

        @on_membrane
        def _():
            collect(1)
            send[0] = message(0)

        for r in range(NB):
            rounded[r] = source[r * TILE : (r + 1) * TILE].astype(BF16)
        east[...] = rounded[NB - 1]
        west[...] = rounded[0]
        north[...] = rounded[1]
        south[...] = rounded[NB - 2]


def update(turn, scaled, args):
    first, last = turn == 0, turn == MATVECS
    if last:
        out = [jax.ShapeDtypeStruct((ROWS, S), F32)]
    else:
        out = [jax.ShapeDtypeStruct((NB, TILE, S), BF16)]
        out += [jax.ShapeDtypeStruct((TILE, S), BF16)] * 4
        out += [jax.ShapeDtypeStruct((GROUPS, GY_N, MESSAGE, S), BF16)]
    if not first:
        out += [jax.ShapeDtypeStruct((1, S), F32)]
    if turn == 1:
        out += [jax.ShapeDtypeStruct((SLOTS, S), F32)]
    scratch = [pltpu.VMEM((MEMB * GY_N, DOFS, CAP, S), F32)]
    if not first and not last:
        scratch += [pltpu.VMEM((ROWS, S), F32)]
    return pl.pallas_call(
        functools.partial(update_kernel, turn, scaled),
        out_shape=out,
        in_specs=[SMEM] + [VMEM] * (len(args) - 1),
        out_specs=[VMEM] * len(out),
        scratch_shapes=scratch,
        compiler_params=pltpu.CompilerParams(vmem_limit_bytes=32 * 1024 * 1024),
        name="update",
    )(*args)


def product_kernel(columns, blocks, rounded, west, east, south, north, out, extended):
    r = pl.program_id(0)

    @pl.when(r == 0)
    def _():
        extended[:NB] = rounded[...]
        extended[NB] = west[...]
        extended[NB + 1] = east[...]
        extended[NB + 2] = south[...]
        extended[NB + 3] = north[...]

    total = dot(blocks[0, 0], extended[columns[r, 0]])
    for k in range(1, KB):
        total += dot(blocks[0, k], extended[columns[r, k]])
    out[...] = total


def product(columns, blocks, rounded, west, east, south, north):
    return pl.pallas_call(
        product_kernel,
        out_shape=jax.ShapeDtypeStruct((ROWS, S), F32),
        grid=(NB,),
        in_specs=[
            SMEM,
            pl.BlockSpec((1, KB, TILE, TILE), lambda r: (r, 0, 0, 0)),
            VMEM,
            VMEM,
            VMEM,
            VMEM,
            VMEM,
        ],
        out_specs=pl.BlockSpec((TILE, S), lambda r: (r, 0)),
        scratch_shapes=[pltpu.VMEM((NB + 4, TILE, S), BF16)],
        compiler_params=pltpu.CompilerParams(vmem_limit_bytes=32 * 1024 * 1024),
        cost_estimate=pl.CostEstimate(
            flops=2 * NB * KB * TILE * TILE * S, bytes_accessed=12_000_000, transcendentals=0
        ),
        name="product",
    )(columns, blocks, rounded, west, east, south, north)


def chain(count, step):
    return [(i, i + step) for i in range(count) if 0 <= i + step < count]


def halos(edges):
    (last, head, second, sixth) = edges
    west = lax.ppermute(last, "gx", chain(GX_N, 1))
    east = lax.ppermute(head, "gx", chain(GX_N, -1))
    south = lax.ppermute(second, "gy", chain(GY_N, 1))
    north = lax.ppermute(sixth, "gy", chain(GY_N, -1))
    return (west, east, south, north)


def total_of(rows):
    count = rows.shape[0]
    spread = jnp.broadcast_to(rows.reshape(1, count * S), (DEVICES, count * S))
    gathered = lax.all_to_all(spread, EVERY, split_axis=0, concat_axis=0, tiled=True)
    return jnp.sum(gathered, axis=0).reshape(count, S)


def exchange(send):
    return lax.all_to_all(
        send.reshape(GROUPS * GY_N, MESSAGE, S),
        ("group", "gy"),
        split_axis=0,
        concat_axis=0,
        tiled=True,
    ).reshape(GROUPS, GY_N, MESSAGE, S)


def split(values):
    high = lax.reduce_precision(values, 8, 7)
    middle = lax.reduce_precision(values - high, 8, 7)
    return jnp.stack([high, middle, values - high - middle], axis=-1).astype(BF16)


def local(start_vectors, tile_blocks, block_columns, sleeve_rod, sleeve_membrane, sleeve_stiffness):
    group = lax.axis_index("group")
    is_rod = group == 0
    memb = jnp.maximum(group - 1, 0)
    blocks = tile_blocks[0, 0, 0]
    columns = block_columns[0, 0, 0]

    rod_nodes = sleeve_rod[0, 0].reshape(SLOTS)
    memb_nodes = lax.dynamic_index_in_dim(
        sleeve_membrane[0, :, :, 0, :], memb, axis=1, keepdims=False
    ).reshape(MSLOTS)
    rest = SLOTS - MSLOTS
    memb_nodes = jnp.concatenate([memb_nodes, jnp.full((rest,), -1, jnp.int32)])
    nodes = jnp.where(is_rod, rod_nodes, memb_nodes)
    ids = jnp.arange(NODES, dtype=jnp.int32)
    gather = (nodes[:, None] == ids[None, :]).astype(BF16)
    scatter = (ids[:, None] == nodes[None, :]).astype(BF16)
    rod_flag = is_rod.astype(jnp.int32).reshape(1)

    stiff = sleeve_stiffness[0, :, :, 0, :]
    pieces = split(stiff)
    low = pieces[:, :DOFS].reshape(GY_N, MESSAGE, 3)
    high = jnp.pad(pieces[:, DOFS], ((0, 0), (0, MESSAGE - CAP), (0, 0)))
    stiff_message = jnp.pad(jnp.concatenate([low, high], axis=2), ((0, 0), (0, 0), (0, S - 6)))
    kappa = lax.dynamic_index_in_dim(stiff, memb, axis=1, keepdims=False).reshape(MSLOTS)
    kappa = jnp.concatenate([kappa, jnp.zeros((rest,), F32)])
    kappa = jnp.broadcast_to(kappa[:, None], (SLOTS, S))

    def step(turn, state, kappa, inverse=None):
        (rounded, *edges, send) = state[:6]
        received = exchange(send)
        base = product(columns, blocks, rounded, *halos(edges))
        args = [rod_flag, base, received, send, kappa, scatter]
        if turn < MATVECS:
            args += [gather]
        if inverse is not None:
            args += [inverse]
        return update(turn, inverse is not None, args)

    start = start_vectors[0, 0, 0].reshape(ROWS, S)
    state = update(0, False, [rod_flag, start, stiff_message, gather])
    state = once = step(1, state, kappa)
    kappa = once[7]
    state = twice = step(2, state, kappa)
    (value, last) = step(3, state, kappa)

    sums = total_of(jnp.concatenate([once[6], twice[6], last], axis=0)) / ALL_DOFS
    safe = jnp.all((sums > LOWEST) & (sums < HIGHEST))
    first_norm = jnp.sqrt(sums[0:1] + EPS)

    def quick(_):
        second_norm = jnp.sqrt(sums[1:2] / jnp.square(first_norm) + EPS)
        both = first_norm * second_norm
        third_norm = jnp.sqrt(sums[2:3] / jnp.square(both) + EPS)
        final = value * (1.0 / (both * third_norm))
        return (final, jnp.concatenate([first_norm, second_norm, third_norm], axis=0))

    def careful(_):
        state = step(2, once, kappa, 1.0 / first_norm)
        second_norm = jnp.sqrt(total_of(state[6]) / ALL_DOFS + EPS)
        (value, squares) = step(3, state, kappa, 1.0 / second_norm)
        third_norm = jnp.sqrt(total_of(squares) / ALL_DOFS + EPS)
        norms = jnp.concatenate([first_norm, second_norm, third_norm], axis=0)
        return (value / third_norm, norms)

    (final, norms) = lax.cond(safe, quick, careful, None)
    return (final.reshape(1, 1, 1, NB, TILE, S), norms)


def solution(mesh):
    spread = ("group", "gx", "gy")
    return jax.shard_map(
        local,
        mesh=mesh,
        in_specs=(
            P(*spread, None, None, None),
            P(*spread, None, None, None, None),
            P(*spread, None, None),
            P("gx", "gy", None, None, None),
            P("gx", None, None, "gy", None),
            P("gx", None, None, "gy", None),
        ),
        out_specs=(P(*spread, None, None, None), P()),
        check_vma=False,
    )
```

time: 217 us -> 182 us (0.84)
  blocking collectives: 65.5 us -> 30.5 us
  waiting for transfers between devices: 7.48 us -> 40.1 us
  starting transfers between devices: 88.3 us -> 61.3 us
  local copies, waits for them, and re-layouts: 26.3 us -> 7.96 us
  Pallas kernels: 18.3 us -> 34.7 us
  other arithmetic: 8.02 us -> 4.45 us
    ppermute x18 -> x12, waiting for transfers between devices: 3.08 us -> 40.1 us  [the longest x3 24.1 us: halos(): south = lax.ppermute(second, 'gy', chain(GY_N, 1))]
    all_to_all x3 -> x1, blocking collectives: 65.5 us -> 30.5 us  [total_of(): lax.all_to_all(spread, EVERY, split_axis=0, concat_axis=0, tiled=True)]
    ppermute x18 -> x12, starting transfers between devices: 52.6 us -> 27.2 us  [the longest x3 9.87 us: halos(): south = lax.ppermute(second, 'gy', chain(GY_N, 1))]
    unnamed x48 -> x44, local copies, waits for them, and re-layouts: 19.6 us -> 5.54 us
    pallas_call x3, Pallas kernels: 13.7 us -> 23.7 us  [product(): pl.pallas_call(product_kernel, out_shape=jax.ShapeDtypeStruct((ROWS, S),...]
    pallas_call x4, Pallas kernels: 4.52 us -> 11 us  [update(): pl.pallas_call(functools.partial(update_kernel, turn, scaled), out_shape=...]
    all_to_all x4 -> x3, waiting for transfers between devices: 4.4 us -> 0.01 us  [exchange(): lax.all_to_all(send.reshape(GROUPS * GY_N, MESSAGE, S), ('group', 'gy'),...]
    div x1, other arithmetic: 2.66 us -> 0.01 us  [local(): total_of(jnp.concatenate([once[6], twice[6], last], axis=0)) / ALL_DOFS]
  transfers between devices with their start and end apart: 22 -> 15, of which waited for: 6 -> 6; matrix products, arithmetic and copies ran while one was open for 3% -> 1% of each run, Pallas kernels for 6% -> 13%
where the time goes in v2:
time: 182 us; the launch traced here: 181 us
  starting transfers between devices  61.3 us (34%)
  waiting for transfers between devices  40.1 us (22%)
  Pallas kernels  34.7 us (19%)
  blocking collectives  30.5 us (17%)
  local copies, waits for them, and re-layouts  7.96 us (4%)
  other arithmetic  4.45 us (2%)
  between operations  1.82 us (1%)
    all_to_all x3, starting transfers between devices, exchange(): lax.all_to_all(send.reshape(GROUPS * GY_N, MESSAGE, S), ('group', 'gy'),...  34.2 us
    all_to_all x1, blocking collectives, total_of(): lax.all_to_all(spread, EVERY, split_axis=0, concat_axis=0, tiled=True)  30.5 us
    ppermute x3, waiting for transfers between devices, halos(): south = lax.ppermute(second, 'gy', chain(GY_N, 1))  24.1 us
    pallas_call x3, Pallas kernels, product(): pl.pallas_call(product_kernel, out_shape=jax.ShapeDtypeStruct((ROWS, S),...  23.7 us
    ppermute x3, waiting for transfers between devices, halos(): north = lax.ppermute(sixth, 'gy', chain(GY_N, -1))  16 us
    pallas_call x4, Pallas kernels, update(): pl.pallas_call(functools.partial(update_kernel, turn, scaled), out_shape=...  11 us
    ppermute x3, starting transfers between devices, halos(): south = lax.ppermute(second, 'gy', chain(GY_N, 1))  9.87 us
    ppermute x3, starting transfers between devices, halos(): west = lax.ppermute(last, 'gx', chain(GX_N, 1))  9.36 us
  transfers between devices with their start and end apart: 15, of which 6 were waited for; matrix products, arithmetic and copies ran while one was open for 1% of the time, Pallas kernels for 13%

profile of v2, /device:TPU:1, one launch (start us, length us, event | category | flops | bytes accessed | tf_op | source)
XLA Modules:
  0.0 180.9 jit_solution(947342453592903438)
XLA Ops:
  2.9 1.5 copy-done.1
  4.5 1.2 update.8
  5.7 13.3 %all-to-all-start.4 = ((bf16[64,48,128]{2,1,0:T(8,128)(2,1)}), bf16[64,48,128]{2,1,0:T(8,128)(2,1)S(1)}, u32[]{:S(2)}, u32[]{:S(2)}) async-start(bf16[64,48,128]{2,1,0:T(8,128)(2,1)} %bitcast.22), calls=%async_computation.4 | async-start | bytes 1572864 | tf_op jit(solution)/shard_map/all_to_all | solution.py:258
  19.0 3.1 %collective-permute-start.8 = (bf16[384,128]{1,0:T(8,128)(2,1)S(1)}, bf16[384,128]{1,0:T(8,128)(2,1)S(1)}, u32[]{:S(2)}, u32[]{:S(2)}) collective-permute-start(bf16[384,128]{1,0:T(8,128)(2,1)S(1)} %get-tuple-element.86), channel_id=1, source_target_pairs={{0,8},{8,16},{16,24},{1,9},{9,17},{17,25},{2,10},{10,18},{18,26},{... | collective-permute-start | bytes 294920 | tf_op jit(solution)/shard_map/ppermute | solution.py:243
  22.1 1.3 collective-permute-start.9
  23.4 3.3 %collective-permute-start.10 = (bf16[384,128]{1,0:T(8,128)(2,1)S(1)}, bf16[384,128]{1,0:T(8,128)(2,1)S(1)}, u32[]{:S(2)}, u32[]{:S(2)}) collective-permute-start(bf16[384,128]{1,0:T(8,128)(2,1)S(1)} %get-tuple-element.88), channel_id=1, source_target_pairs={{0,1},{1,2},{2,3},{3,4},{4,5},{5,6},{6,7},{8,9},{9,10},{10,11},{11... | collective-permute-start | bytes 294920 | tf_op jit(solution)/shard_map/ppermute | solution.py:245
  26.7 1.3 collective-permute-start.11
  29.9 6.9 %collective-permute-done.10.south = bf16[384,128]{1,0:T(8,128)(2,1)S(1)} collective-permute-done((bf16[384,128]{1,0:T(8,128)(2,1)S(1)}, bf16[384,128]{1,0:T(8,128)(2,1)S(1)}, u32[]{:S(2)}, u32[]{:S(2)}) %collective-permute-start.10) | collective-permute-done | bytes 98336 | tf_op jit(solution)/shard_map/ppermute | solution.py:245
  36.8 5.3 %collective-permute-done.11.north = bf16[384,128]{1,0:T(8,128)(2,1)S(1)} collective-permute-done((bf16[384,128]{1,0:T(8,128)(2,1)S(1)}, bf16[384,128]{1,0:T(8,128)(2,1)S(1)}, u32[]{:S(2)}, u32[]{:S(2)}) %collective-permute-start.11) | collective-permute-done | bytes 98336 | tf_op jit(solution)/shard_map/ppermute | solution.py:246
  43.6 7.9 %product.7.refs_1_ = f32[3072,128]{1,0:T(8,128)S(1)} custom-call(s32[8,4]{1,0:T(8,128)S(1)} %copy.41.columns, bf16[8,4,384,384]{3,2,1,0:T(8,128)(2,1)} %bitcast.63, bf16[8,384,128]{2,1,0:T(8,128)(2,1)S(1)} %get-tuple-element.85.rounded, bf16[384,128]{1,0:T(8,128)(2,1)S(1)} %collective-permute-done.8.west, bf16[384,128]{1,0:T(8,128)(2,1)S(1)} %collective-permute-done.9.east, ...), custom_call_target="tpu_custom_call" | custom-call | flops 1207959552 | bytes 12000000 | tf_op jit(solution)/shard_map/product/pallas_call | solution.py:214
  51.6 3.4 %update.9 = (bf16[8,384,128]{2,1,0:T(8,128)(2,1)S(1)}, bf16[384,128]{1,0:T(8,128)(2,1)S(1)}, bf16[384,128]{1,0:T(8,128)(2,1)S(1)}, bf16[384,128]{1,0:T(8,128)(2,...) custom-call(s32[1]{0:T(128)} %bitcast.16.refs_0_, ...), custom_call_target="tpu_custom_call" | custom-call | tf_op jit(solution)/shard_map/update/pallas_call | solution.py:185
  55.1 10.4 %all-to-all-start.5 = ((bf16[64,48,128]{2,1,0:T(8,128)(2,1)}), bf16[64,48,128]{2,1,0:T(8,128)(2,1)S(1)}, u32[]{:S(2)}, u32[]{:S(2)}) async-start(bf16[64,48,128]{2,1,0:T(8,128)(2,1)} %bitcast.24), calls=%async_computation.5 | async-start | bytes 1572864 | tf_op jit(solution)/shard_map/all_to_all | solution.py:258
  65.5 3.1 %collective-permute-start.12 = (bf16[384,128]{1,0:T(8,128)(2,1)S(1)}, bf16[384,128]{1,0:T(8,128)(2,1)S(1)}, u32[]{:S(2)}, u32[]{:S(2)}) collective-permute-start(bf16[384,128]{1,0:T(8,128)(2,1)S(1)} %get-tuple-element.93), channel_id=1, source_target_pairs={{0,8},{8,16},{16,24},{1,9},{9,17},{17,25},{2,10},{10,18},{18,26},{... | collective-permute-start | bytes 294920 | tf_op jit(solution)/shard_map/ppermute | solution.py:243
  68.6 1.3 collective-permute-start.13
  70.0 3.3 %collective-permute-start.14 = (bf16[384,128]{1,0:T(8,128)(2,1)S(1)}, bf16[384,128]{1,0:T(8,128)(2,1)S(1)}, u32[]{:S(2)}, u32[]{:S(2)}) collective-permute-start(bf16[384,128]{1,0:T(8,128)(2,1)S(1)} %copy-done.24), channel_id=1, source_target_pairs={{0,1},{1,2},{2,3},{3,4},{4,5},{5,6},{6,7},{8,9},{9,10},{10,11},{11... | collective-permute-start | bytes 294920 | tf_op jit(solution)/shard_map/ppermute | solution.py:245
  73.3 1.3 collective-permute-start.15
  74.6 8.7 %collective-permute-done.14.south = bf16[384,128]{1,0:T(8,128)(2,1)S(1)} collective-permute-done((bf16[384,128]{1,0:T(8,128)(2,1)S(1)}, bf16[384,128]{1,0:T(8,128)(2,1)S(1)}, u32[]{:S(2)}, u32[]{:S(2)}) %collective-permute-start.14) | collective-permute-done | bytes 98336 | tf_op jit(solution)/shard_map/ppermute | solution.py:245
  83.3 5.3 %collective-permute-done.15.north = bf16[384,128]{1,0:T(8,128)(2,1)S(1)} collective-permute-done((bf16[384,128]{1,0:T(8,128)(2,1)S(1)}, bf16[384,128]{1,0:T(8,128)(2,1)S(1)}, u32[]{:S(2)}, u32[]{:S(2)}) %collective-permute-start.15) | collective-permute-done | bytes 98336 | tf_op jit(solution)/shard_map/ppermute | solution.py:246
  88.6 7.9 %product.8.refs_1_ = f32[3072,128]{1,0:T(8,128)S(1)} custom-call(s32[8,4]{1,0:T(8,128)S(1)} %copy.41.columns, bf16[8,4,384,384]{3,2,1,0:T(8,128)(2,1)} %bitcast.64, bf16[8,384,128]{2,1,0:T(8,128)(2,1)S(1)} %get-tuple-element.92.rounded, bf16[384,128]{1,0:T(8,128)(2,1)S(1)} %collective-permute-done.12.west, ...), custom_call_target="tpu_custom_call" | custom-call | flops 1207959552 | bytes 12000000 | tf_op jit(solution)/shard_map/product/pallas_call | solution.py:214
  96.5 3.3 %update.10 = (bf16[8,384,128]{2,1,0:T(8,128)(2,1)S(1)}, bf16[384,128]{1,0:T(8,128)(2,1)S(1)}, bf16[384,128]{1,0:T(8,128)(2,1)S(1)}, bf16[384,128]{1,0:T(8,128)(2...) custom-call(s32[1]{0:T(128)} %bitcast.16.refs_0_, ...), custom_call_target="tpu_custom_call" | custom-call | tf_op jit(solution)/shard_map/update/pallas_call | solution.py:185
  101.1 10.4 %all-to-all-start.6 = ((bf16[64,48,128]{2,1,0:T(8,128)(2,1)}), bf16[64,48,128]{2,1,0:T(8,128)(2,1)S(1)}, u32[]{:S(2)}, u32[]{:S(2)}) async-start(bf16[64,48,128]{2,1,0:T(8,128)(2,1)} %bitcast.26), calls=%async_computation.6 | async-start | bytes 1572864 | tf_op jit(solution)/shard_map/all_to_all | solution.py:258
  111.6 3.1 %collective-permute-start.16 = (bf16[384,128]{1,0:T(8,128)(2,1)S(1)}, bf16[384,128]{1,0:T(8,128)(2,1)S(1)}, u32[]{:S(2)}, u32[]{:S(2)}) collective-permute-start(bf16[384,128]{1,0:T(8,128)(2,1)S(1)} %copy-done.10), channel_id=1, source_target_pairs={{0,8},{8,16},{16,24},{1,9},{9,17},{17,25},{2,10},{10,18},{18,26},{... | collective-permute-start | bytes 294920 | tf_op jit(solution)/shard_map/ppermute | solution.py:243
  114.7 1.3 collective-permute-start.17
  116.0 3.3 %collective-permute-start.18 = (bf16[384,128]{1,0:T(8,128)(2,1)S(1)}, bf16[384,128]{1,0:T(8,128)(2,1)S(1)}, u32[]{:S(2)}, u32[]{:S(2)}) collective-permute-start(bf16[384,128]{1,0:T(8,128)(2,1)S(1)} %get-tuple-element.103), channel_id=1, source_target_pairs={{0,1},{1,2},{2,3},{3,4},{4,5},{5,6},{6,7},{8,9},{9,10},{10,11},{11... | collective-permute-start | bytes 294920 | tf_op jit(solution)/shard_map/ppermute | solution.py:245
  119.3 1.5 collective-permute-start.19
  120.8 8.5 %collective-permute-done.18.south = bf16[384,128]{1,0:T(8,128)(2,1)S(1)} collective-permute-done((bf16[384,128]{1,0:T(8,128)(2,1)S(1)}, bf16[384,128]{1,0:T(8,128)(2,1)S(1)}, u32[]{:S(2)}, u32[]{:S(2)}) %collective-permute-start.18) | collective-permute-done | bytes 98336 | tf_op jit(solution)/shard_map/ppermute | solution.py:245
  129.3 5.3 %collective-permute-done.19.north = bf16[384,128]{1,0:T(8,128)(2,1)S(1)} collective-permute-done((bf16[384,128]{1,0:T(8,128)(2,1)S(1)}, bf16[384,128]{1,0:T(8,128)(2,1)S(1)}, u32[]{:S(2)}, u32[]{:S(2)}) %collective-permute-start.19) | collective-permute-done | bytes 98336 | tf_op jit(solution)/shard_map/ppermute | solution.py:246
  134.7 7.9 %product.9.refs_1_ = f32[3072,128]{1,0:T(8,128)S(1)} custom-call(s32[8,4]{1,0:T(8,128)S(1)} %copy.41.columns, bf16[8,4,384,384]{3,2,1,0:T(8,128)(2,1)} %bitcast.65, bf16[8,384,128]{2,1,0:T(8,128)(2,1)S(1)} %get-tuple-element.100.rounded, bf16[384,128]{1,0:T(8,128)(2,1)S(1)} %collective-permute-done.16.west, ...), custom_call_target="tpu_custom_call" | custom-call | flops 1207959552 | bytes 12000000 | tf_op jit(solution)/shard_map/product/pallas_call | solution.py:214
  142.6 3.0 %update.11 = (f32[3072,128]{1,0:T(8,128)}, f32[1,128]{1,0:T(1,128)S(1)}) custom-call(s32[1]{0:T(128)} %bitcast.16.refs_0_, f32[3072,128]{1,0:T(8,128)S(1)} %product.9.refs_1_, bf16[8,8,48,128]{3,2,1,0:T(8,128)(2,1)S(1)} %bitcast.59, bf16[8,8,48,128]{3,2,1,0:T(8,128)(2,1)} %get-tuple-element.105.refs_3_, f32[448,128]{1,0:T(8,128)S(1)} %copy-done.12, ...), custom_call_target="tpu_custom_call" | custom-call | tf_op jit(solution)/shard_map/update/pallas_call | solution.py:185
  145.9 30.5 %all_to_all.41 = f32[256,1,384]{2,1,0:T(1,128)S(1)} all-to-all(f32[256,1,384]{2,1,0:T(1,128)S(1)} %broadcast_in_dim.12), channel_id=1, replica_groups=mesh['group'=8,'gx'=4,'gy'=8] {'group','gx','gy'}, dimensions={0} | all-to-all | bytes 786432 | tf_op jit(solution)/shard_map/all_to_all | solution.py:253
  178.1 1.6 conditional.1
  178.2 1.5 broadcast_multiply_fusion
  (80 shorter events, 9.4 us)
Async XLA Ops:
  0.6 1.7 copy-start
  2.9 2.8 %copy-start.11 = (bf16[448,512]{1,0:T(8,128)(2,1)}, bf16[448,512]{1,0:T(8,128)(2,1)S(1)}, u32[]{:S(2)}) copy-start(bf16[448,512]{1,0:T(8,128)(2,1)S(1)} %fusion.2.refs_3_.refs_6_) | copy-start | bytes 1376260
  2.9 1.6 copy-start.1
  5.7 23.3 %copy-start.18 = (s32[1,1,1,8,4]{3,4,2,1,0:T(4,128)S(1)}, s32[1,1,1,8,4]{3,4,2,1,0:T(4,128)}, u32[]{:S(2)}) copy-start(s32[1,1,1,8,4]{3,4,2,1,0:T(4,128)} %param.10) | copy-start | bytes 388
  5.7 45.8 %all-to-all-start.4 = ((bf16[64,48,128]{2,1,0:T(8,128)(2,1)}), bf16[64,48,128]{2,1,0:T(8,128)(2,1)S(1)}, u32[]{:S(2)}, u32[]{:S(2)}) async-start(bf16[64,48,128]{2,1,0:T(8,128)(2,1)} %bitcast.22), calls=%async_computation.4 | async-start | bytes 1572864 | tf_op jit(solution)/shard_map/all_to_all | solution.py:258
  19.0 10.8 %collective-permute-start.8 = (bf16[384,128]{1,0:T(8,128)(2,1)S(1)}, bf16[384,128]{1,0:T(8,128)(2,1)S(1)}, u32[]{:S(2)}, u32[]{:S(2)}) collective-permute-start(bf16[384,128]{1,0:T(8,128)(2,1)S(1)} %get-tuple-element.86), channel_id=1, source_target_pairs={{0,8},{8,16},{16,24},{1,9},{9,17},{17,25},{2,10},{10,18},{18,26},{... | collective-permute-start | bytes 294920 | tf_op jit(solution)/shard_map/ppermute | solution.py:243
  22.1 7.7 %collective-permute-start.9 = (bf16[384,128]{1,0:T(8,128)(2,1)S(1)}, bf16[384,128]{1,0:T(8,128)(2,1)S(1)}, u32[]{:S(2)}, u32[]{:S(2)}) collective-permute-start(bf16[384,128]{1,0:T(8,128)(2,1)S(1)} %get-tuple-element.87), channel_id=1, source_target_pairs={{8,0},{16,8},{24,16},{9,1},{17,9},{25,17},{10,2},{18,10},{26,18},{... | collective-permute-start | bytes 294920 | tf_op jit(solution)/shard_map/ppermute | solution.py:244
  23.4 13.3 %collective-permute-start.10 = (bf16[384,128]{1,0:T(8,128)(2,1)S(1)}, bf16[384,128]{1,0:T(8,128)(2,1)S(1)}, u32[]{:S(2)}, u32[]{:S(2)}) collective-permute-start(bf16[384,128]{1,0:T(8,128)(2,1)S(1)} %get-tuple-element.88), channel_id=1, source_target_pairs={{0,1},{1,2},{2,3},{3,4},{4,5},{5,6},{6,7},{8,9},{9,10},{10,11},{11... | collective-permute-start | bytes 294920 | tf_op jit(solution)/shard_map/ppermute | solution.py:245
  26.7 15.4 %collective-permute-start.11 = (bf16[384,128]{1,0:T(8,128)(2,1)S(1)}, bf16[384,128]{1,0:T(8,128)(2,1)S(1)}, u32[]{:S(2)}, u32[]{:S(2)}) collective-permute-start(bf16[384,128]{1,0:T(8,128)(2,1)S(1)} %get-tuple-element.89), channel_id=1, source_target_pairs={{1,0},{2,1},{3,2},{4,3},{5,4},{6,5},{7,6},{9,8},{10,9},{11,10},{12... | collective-permute-start | bytes 294920 | tf_op jit(solution)/shard_map/ppermute | solution.py:246
  55.0 41.5 %copy-start.15 = (bf16[8,384,128]{2,1,0:T(8,128)(2,1)}, bf16[8,384,128]{2,1,0:T(8,128)(2,1)S(1)}, u32[]{:S(2)}) copy-start(bf16[8,384,128]{2,1,0:T(8,128)(2,1)S(1)} %get-tuple-element.92.rounded) | copy-start | bytes 2359300
  55.0 41.5 %copy-start.20 = (bf16[384,128]{1,0:T(8,128)(2,1)}, bf16[384,128]{1,0:T(8,128)(2,1)S(1)}, u32[]{:S(2)}) copy-start(bf16[384,128]{1,0:T(8,128)(2,1)S(1)} %get-tuple-element.93) | copy-start | bytes 294916
  55.0 41.5 %copy-start.22 = (bf16[384,128]{1,0:T(8,128)(2,1)}, bf16[384,128]{1,0:T(8,128)(2,1)S(1)}, u32[]{:S(2)}) copy-start(bf16[384,128]{1,0:T(8,128)(2,1)S(1)} %get-tuple-element.94) | copy-start | bytes 294916
  55.0 14.9 %copy-start.24 = (bf16[384,128]{1,0:T(8,128)(2,1)S(1)}, bf16[384,128]{1,0:T(8,128)(2,1)}, u32[]{:S(2)}) copy-start(bf16[384,128]{1,0:T(8,128)(2,1)} %get-tuple-element.95) | copy-start | bytes 294916
  55.1 18.2 %copy-start.26 = (bf16[384,128]{1,0:T(8,128)(2,1)S(1)}, bf16[384,128]{1,0:T(8,128)(2,1)}, u32[]{:S(2)}) copy-start(bf16[384,128]{1,0:T(8,128)(2,1)} %get-tuple-element.96) | copy-start | bytes 294916
  55.1 41.5 %all-to-all-start.5 = ((bf16[64,48,128]{2,1,0:T(8,128)(2,1)}), bf16[64,48,128]{2,1,0:T(8,128)(2,1)S(1)}, u32[]{:S(2)}, u32[]{:S(2)}) async-start(bf16[64,48,128]{2,1,0:T(8,128)(2,1)} %bitcast.24), calls=%async_computation.5 | async-start | bytes 1572864 | tf_op jit(solution)/shard_map/all_to_all | solution.py:258
  65.5 9.0 %collective-permute-start.12 = (bf16[384,128]{1,0:T(8,128)(2,1)S(1)}, bf16[384,128]{1,0:T(8,128)(2,1)S(1)}, u32[]{:S(2)}, u32[]{:S(2)}) collective-permute-start(bf16[384,128]{1,0:T(8,128)(2,1)S(1)} %get-tuple-element.93), channel_id=1, source_target_pairs={{0,8},{8,16},{16,24},{1,9},{9,17},{17,25},{2,10},{10,18},{18,26},{... | collective-permute-start | bytes 294920 | tf_op jit(solution)/shard_map/ppermute | solution.py:243
  68.6 5.9 %collective-permute-start.13 = (bf16[384,128]{1,0:T(8,128)(2,1)S(1)}, bf16[384,128]{1,0:T(8,128)(2,1)S(1)}, u32[]{:S(2)}, u32[]{:S(2)}) collective-permute-start(bf16[384,128]{1,0:T(8,128)(2,1)S(1)} %get-tuple-element.94), channel_id=1, source_target_pairs={{8,0},{16,8},{24,16},{9,1},{17,9},{25,17},{10,2},{18,10},{26,18},{... | collective-permute-start | bytes 294920 | tf_op jit(solution)/shard_map/ppermute | solution.py:244
  70.0 13.3 %collective-permute-start.14 = (bf16[384,128]{1,0:T(8,128)(2,1)S(1)}, bf16[384,128]{1,0:T(8,128)(2,1)S(1)}, u32[]{:S(2)}, u32[]{:S(2)}) collective-permute-start(bf16[384,128]{1,0:T(8,128)(2,1)S(1)} %copy-done.24), channel_id=1, source_target_pairs={{0,1},{1,2},{2,3},{3,4},{4,5},{5,6},{6,7},{8,9},{9,10},{10,11},{11... | collective-permute-start | bytes 294920 | tf_op jit(solution)/shard_map/ppermute | solution.py:245
  73.3 15.3 %collective-permute-start.15 = (bf16[384,128]{1,0:T(8,128)(2,1)S(1)}, bf16[384,128]{1,0:T(8,128)(2,1)S(1)}, u32[]{:S(2)}, u32[]{:S(2)}) collective-permute-start(bf16[384,128]{1,0:T(8,128)(2,1)S(1)} %copy-done.26), channel_id=1, source_target_pairs={{1,0},{2,1},{3,2},{4,3},{5,4},{6,5},{7,6},{9,8},{10,9},{11,10},{12... | collective-permute-start | bytes 294920 | tf_op jit(solution)/shard_map/ppermute | solution.py:246
  101.1 10.5 %copy-start.10 = (bf16[384,128]{1,0:T(8,128)(2,1)S(1)}, bf16[384,128]{1,0:T(8,128)(2,1)}, u32[]{:S(2)}) copy-start(bf16[384,128]{1,0:T(8,128)(2,1)} %copy-done.9) | copy-start | bytes 294916
  101.1 13.6 %copy-start.8 = (bf16[384,128]{1,0:T(8,128)(2,1)S(1)}, bf16[384,128]{1,0:T(8,128)(2,1)}, u32[]{:S(2)}) copy-start(bf16[384,128]{1,0:T(8,128)(2,1)} %copy-done.7) | copy-start | bytes 294916
  101.1 41.5 %all-to-all-start.6 = ((bf16[64,48,128]{2,1,0:T(8,128)(2,1)}), bf16[64,48,128]{2,1,0:T(8,128)(2,1)S(1)}, u32[]{:S(2)}, u32[]{:S(2)}) async-start(bf16[64,48,128]{2,1,0:T(8,128)(2,1)} %bitcast.26), calls=%async_computation.6 | async-start | bytes 1572864 | tf_op jit(solution)/shard_map/all_to_all | solution.py:258
  111.6 9.2 %collective-permute-start.16 = (bf16[384,128]{1,0:T(8,128)(2,1)S(1)}, bf16[384,128]{1,0:T(8,128)(2,1)S(1)}, u32[]{:S(2)}, u32[]{:S(2)}) collective-permute-start(bf16[384,128]{1,0:T(8,128)(2,1)S(1)} %copy-done.10), channel_id=1, source_target_pairs={{0,8},{8,16},{16,24},{1,9},{9,17},{17,25},{2,10},{10,18},{18,26},{... | collective-permute-start | bytes 294920 | tf_op jit(solution)/shard_map/ppermute | solution.py:243
  114.7 6.1 %collective-permute-start.17 = (bf16[384,128]{1,0:T(8,128)(2,1)S(1)}, bf16[384,128]{1,0:T(8,128)(2,1)S(1)}, u32[]{:S(2)}, u32[]{:S(2)}) collective-permute-start(bf16[384,128]{1,0:T(8,128)(2,1)S(1)} %copy-done.8), channel_id=1, source_target_pairs={{8,0},{16,8},{24,16},{9,1},{17,9},{25,17},{10,2},{18,10},{26,18},{... | collective-permute-start | bytes 294920 | tf_op jit(solution)/shard_map/ppermute | solution.py:244
  116.0 13.3 %collective-permute-start.18 = (bf16[384,128]{1,0:T(8,128)(2,1)S(1)}, bf16[384,128]{1,0:T(8,128)(2,1)S(1)}, u32[]{:S(2)}, u32[]{:S(2)}) collective-permute-start(bf16[384,128]{1,0:T(8,128)(2,1)S(1)} %get-tuple-element.103), channel_id=1, source_target_pairs={{0,1},{1,2},{2,3},{3,4},{4,5},{5,6},{6,7},{8,9},{9,10},{10,11},{11... | collective-permute-start | bytes 294920 | tf_op jit(solution)/shard_map/ppermute | solution.py:245
  119.3 15.3 %collective-permute-start.19 = (bf16[384,128]{1,0:T(8,128)(2,1)S(1)}, bf16[384,128]{1,0:T(8,128)(2,1)S(1)}, u32[]{:S(2)}, u32[]{:S(2)}) collective-permute-start(bf16[384,128]{1,0:T(8,128)(2,1)S(1)} %get-tuple-element.104), channel_id=1, source_target_pairs={{1,0},{2,1},{3,2},{4,3},{5,4},{6,5},{7,6},{9,8},{10,9},{11,10},{12... | collective-permute-start | bytes 294920 | tf_op jit(solution)/shard_map/ppermute | solution.py:246
  134.7 7.9 %copy-start.12 = (f32[448,128]{1,0:T(8,128)S(1)}, f32[448,128]{1,0:T(8,128)}, u32[]{:S(2)}) copy-start(f32[448,128]{1,0:T(8,128)} %get-tuple-element.98.refs_4_) | copy-start | bytes 688132
  145.6 32.5 %copy-start.21 = (bf16[384,128]{1,0:T(8,128)(2,1)S(1)}, bf16[384,128]{1,0:T(8,128)(2,1)}, u32[]{:S(2)}) copy-start(bf16[384,128]{1,0:T(8,128)(2,1)} %copy-done.20) | copy-start | bytes 294916
  145.6 32.5 %copy-start.23 = (bf16[384,128]{1,0:T(8,128)(2,1)S(1)}, bf16[384,128]{1,0:T(8,128)(2,1)}, u32[]{:S(2)}) copy-start(bf16[384,128]{1,0:T(8,128)(2,1)} %copy-done.22) | copy-start | bytes 294916
  145.6 32.5 %copy-start.25 = (bf16[384,128]{1,0:T(8,128)(2,1)S(1)}, bf16[384,128]{1,0:T(8,128)(2,1)}, u32[]{:S(2)}) copy-start(bf16[384,128]{1,0:T(8,128)(2,1)} %get-tuple-element.95) | copy-start | bytes 294916
  145.6 32.5 %copy-start.27 = (bf16[384,128]{1,0:T(8,128)(2,1)S(1)}, bf16[384,128]{1,0:T(8,128)(2,1)}, u32[]{:S(2)}) copy-start(bf16[384,128]{1,0:T(8,128)(2,1)} %get-tuple-element.96) | copy-start | bytes 294916
  179.7 1.1 copy-start.16
  (5 other events, 3.9 us)
